TPU v7x, 32 devices: a whole 2x2x4 slice. The times are simulated.
32 devices in a mesh: layer: 4 (over x, core), proc: 8 (over z, y).
Axes of the slice: x: 2, y: 2, z: 4, core: 2. Of those that a mesh axis runs over, the one named last changes fastest.
Arguments:
- owner: int32 [4, 6], P('layer'), may hold values from 0 to 7
- rhs_blocks: bfloat16 [8192, 256], P(('layer', 'proc')), may hold values from -6 to 6
- chain_blocks: bfloat16 [8192, 256], P(('layer', 'proc')), may hold values from -0.1875 to 0.1875
- diag_inverse: bfloat16 [8192, 256], P(('layer', 'proc')), may hold values from -1 to 2
- factor_blocks: bfloat16 [655360, 256], P(('layer', 'proc')), may hold values from -0.015625 to 0.015625
- col_index: int32 [32, 80], P(('layer', 'proc')), may hold values from 0 to 5
- row_index: int32 [32, 80], P(('layer', 'proc')), may hold values from 0 to 3
- anc_rhs: float32 [1024, 256], P(None, 'proc'), may hold values from -6 to 6
- anc_inverse: bfloat16 [1024, 256], replicated, may hold values from -1 to 2
Outputs:
- solved: bfloat16 [6144, 256], P('layer', 'proc')
- ancestor: float32 [1024, 256], P(None, 'proc')
All inputs are finite; a program needn't handle non-finite values.
Results may differ from a plain program's by a relative error of at most 0.006.
Values may be sent and summed in bfloat16 or wider, within the bound.
No kernel may reach another device: no remote copies, remote signals or barrier semaphores. Data moves between devices by JAX's collectives and lax.ppermute only.
A program may use at most 128 MiB of HBM per device.

v0:
```python
import jax
import jax.numpy as jnp
from jax import lax
from jax.sharding import PartitionSpec as P


def broadcast(block, axis, owner):
    block = jnp.where(lax.axis_index(axis) == owner, block, jnp.zeros_like(block))
    return lax.psum(block, axis)


def per_device(
    owner,
    rhs_blocks,
    chain_blocks,
    diag_inverse,
    factor_blocks,
    col_index,
    row_index,
    anc_rhs,
    anc_inverse,
):
    owners = owner[0]
    tick_count = owners.shape[0]
    block_size = chain_blocks.shape[1]
    rhs_width = rhs_blocks.shape[1]
    anc_rows = anc_inverse.shape[0]
    anc_count = anc_rows // block_size
    factor_count = col_index.shape[1]
    previous = jnp.zeros((block_size, rhs_width), jnp.bfloat16)
    solved_ticks = []
    for tick_index in range(tick_count):
        reduced = rhs_blocks.astype(jnp.float32) - jnp.dot(
            chain_blocks, previous, preferred_element_type=jnp.float32
        )
        candidate = jnp.dot(
            diag_inverse, reduced.astype(jnp.bfloat16), preferred_element_type=jnp.float32
        ).astype(jnp.bfloat16)
        previous = broadcast(candidate, "proc", owners[tick_index])
        solved_ticks.append(previous)
    stacked = jnp.stack(solved_ticks)
    col_hot = (col_index[0][:, None] == jnp.arange(tick_count)[None, :]).astype(jnp.bfloat16)
    row_hot = (row_index[0][:, None] == jnp.arange(anc_count)[None, :]).astype(jnp.bfloat16)
    pair_hot = (row_hot[:, :, None] * col_hot[:, None, :]).reshape(
        factor_count, anc_count * tick_count
    )
    grouped = jnp.dot(
        pair_hot.T,
        factor_blocks.reshape(factor_count, block_size * block_size),
        preferred_element_type=jnp.float32,
    ).reshape(anc_count, tick_count, block_size, block_size)
    partial_value = jnp.einsum(
        "atbc,tcr->abr", grouped, stacked.astype(jnp.float32), precision=lax.Precision.HIGHEST
    ).reshape(anc_rows, rhs_width)
    share_sum = lax.psum_scatter(partial_value, "layer", scatter_dimension=0, tiled=True)
    share_sum = lax.psum_scatter(share_sum, "proc", scatter_dimension=1, tiled=True)
    summed = lax.all_gather(share_sum, "layer", axis=0, tiled=True)
    columns = summed.shape[1]
    remaining = (anc_rhs - summed).astype(jnp.bfloat16).reshape(anc_count, block_size, columns)
    inverse = anc_inverse.reshape(anc_count, block_size, block_size)
    ancestor = jnp.einsum(
        "abc,acr->abr", inverse, remaining, preferred_element_type=jnp.float32
    ).reshape(anc_rows, columns)
    start_col = lax.axis_index("proc") * columns
    solved = lax.dynamic_slice_in_dim(stacked, start_col, columns, 2).reshape(
        tick_count * block_size, columns
    )
    return (solved, ancestor)


def solution(mesh):
    placed = (
        P("layer", None),
        P(("layer", "proc"), None),
        P(("layer", "proc"), None),
        P(("layer", "proc"), None),
        P(("layer", "proc"), None),
        P(("layer", "proc"), None),
        P(("layer", "proc"), None),
        P(None, "proc"),
        P(),
    )
    return jax.shard_map(
        per_device,
        mesh=mesh,
        in_specs=placed,
        out_specs=(P("layer", "proc"), P(None, "proc")),
        check_vma=False,
    )
```

profile of v0, /device:TPU:0, one launch (start us, length us, event | category | flops | bytes accessed | tf_op | source)
XLA Modules:
  0.0 561.7 jit_solution(10208686298960038719)
XLA Ops:
  7.2 0.0 copy-start
  7.2 0.0 all-reduce.7.cloned.1.call-start
  7.2 1.5 fusion.44
  9.4 2.1 fusion.17
  11.5 0.0 all-reduce.7.cloned.1.call-update
  11.5 0.0 all-reduce.9.cloned.1.call-start
  11.6 13.0 %reshape.88 = bf16[80,65536]{1,0:T(8,128)(2,1)} reshape(bf16[20480,256]{1,0:T(8,128)(2,1)} %param.13) | data formatting | bytes 20971520 | tf_op jit(solution)/shard_map/reshape | solution.py:49
  24.6 10.9 %copy.28 = bf16[10,8,256,256]{3,2,1,0:T(8,128)(2,1)} copy(bf16[10,8,256,256]{3,1,2,0:T(8,128)(2,1)} %bitcast.154) | data formatting | bytes 20971520
  35.6 13.5 %fusion = f32[4,6,256,256]{3,1,2,0:T(8,128)} fusion(bf16[256,256,80,1]{1,0,2,3:T(8,128)(2,1)} %bitcast.155, bf16[4,6,80,1]{2,1,0,3:T(8,128)(2,1)S(1)} %reshape.93), kind=kOutput, calls=%fused_computation | convolution fusion | flops 251658240 | bytes 16781056 | tf_op jit(solution)/shard_map/dot_general | solution.py:47
  52.2 32.1 %all-reduce.7.cloned.1.call-done = bf16[256,256]{0,1:T(8,128)(2,1)} async-done(((bf16[256,256]{0,1:T(8,128)(2,1)}), bf16[256,256]{0,1:T(8,128)(2,1)}) %all-reduce.7.cloned.1.call-update) | async-done | bytes 131088 | tf_op jit(solution)/shard_map/psum | solution.py:9
  84.3 2.0 fusion.27
  86.4 0.0 all-reduce.9.cloned.1.call-update
  86.4 0.0 all-reduce.11.cloned.1.call-start
  86.4 0.9 bitcast_dynamic-update-slice_fusion.4
  87.4 70.2 %all-reduce.9.cloned.1.call-done = bf16[256,256]{0,1:T(8,128)(2,1)} async-done(((bf16[256,256]{0,1:T(8,128)(2,1)}), bf16[256,256]{0,1:T(8,128)(2,1)}) %all-reduce.9.cloned.1.call-update) | async-done | bytes 131088 | tf_op jit(solution)/shard_map/psum | solution.py:9
  157.5 2.0 fusion.25
  159.5 0.0 all-reduce.11.cloned.1.call-update
  159.6 0.0 all-reduce.13.cloned.1.call-start
  159.6 0.9 bitcast_dynamic-update-slice_fusion.3
  160.5 69.8 %all-reduce.11.cloned.1.call-done = bf16[256,256]{0,1:T(8,128)(2,1)} async-done(((bf16[256,256]{0,1:T(8,128)(2,1)}), bf16[256,256]{0,1:T(8,128)(2,1)}) %all-reduce.11.cloned.1.call-update) | async-done | bytes 131088 | tf_op jit(solution)/shard_map/psum | solution.py:9
  230.3 2.0 fusion.23
  232.4 0.0 all-reduce.13.cloned.1.call-update
  232.4 0.0 all-reduce.15.cloned.1.call-start
  232.4 0.9 bitcast_dynamic-update-slice_fusion.2
  233.4 70.0 %all-reduce.13.cloned.1.call-done = bf16[256,256]{0,1:T(8,128)(2,1)} async-done(((bf16[256,256]{0,1:T(8,128)(2,1)}), bf16[256,256]{0,1:T(8,128)(2,1)}) %all-reduce.13.cloned.1.call-update) | async-done | bytes 131088 | tf_op jit(solution)/shard_map/psum | solution.py:9
  303.4 2.0 fusion.21
  305.4 0.0 all-reduce.15.cloned.1.call-update
  305.4 0.0 all-reduce.17.cloned.1.call-start
  305.5 0.9 bitcast_dynamic-update-slice_fusion.1
  306.4 69.7 %all-reduce.15.cloned.1.call-done = bf16[256,256]{0,1:T(8,128)(2,1)} async-done(((bf16[256,256]{0,1:T(8,128)(2,1)}), bf16[256,256]{0,1:T(8,128)(2,1)}) %all-reduce.15.cloned.1.call-update) | async-done | bytes 131088 | tf_op jit(solution)/shard_map/psum | solution.py:9
  376.1 2.0 fusion.19
  378.1 0.0 all-reduce.17.cloned.1.call-update
  378.1 0.2 reduce-scatter.3.cloned.1.call-start
  378.4 0.9 bitcast_dynamic-update-slice_fusion
  379.3 69.8 %all-reduce.17.cloned.1.call-done = bf16[1,256,256]{1,2,0:T(8,128)(2,1)} async-done(((bf16[1,256,256]{1,2,0:T(8,128)(2,1)}), bf16[1,256,256]{1,2,0:T(8,128)(2,1)}) %all-reduce.17.cloned.1.call-update) | async-done | bytes 131088 | tf_op jit(solution)/shard_map/psum | solution.py:9
  449.1 0.9 constant_dynamic-update-slice_fusion
  450.0 7.7 %fusion.2 = f32[4,256,256,1]{2,1,3,0:T(8,128)S(1)} fusion(f32[4,6,256,256]{3,1,2,0:T(8,128)} %fusion, bf16[6,256,256]{1,2,0:T(8,128)(2,1)S(1)} %constant_dynamic-update-slice_fusion), kind=kOutput, calls=%fused_computation.2 | convolution fusion | flops 4831838208 | bytes 8126464 | tf_op jit(solution)/shard_map/atbc,tcr->abr/dot_general | solution.py:52
  457.7 1.3 copy.16
  459.0 0.0 reduce-scatter.3.cloned.1.call-update
  459.1 0.0 reduce-scatter.5.cloned.1.call-start
  459.1 24.3 %reduce-scatter.3.cloned.1.call-done = f32[256,256]{0,1:T(8,128)} async-done(((f32[1024,256]{0,1:T(8,128)}), f32[256,256]{0,1:T(8,128)}) %reduce-scatter.3.cloned.1.call-update) | async-done | bytes 262160 | tf_op jit(solution)/shard_map/reduce_scatter | solution.py:55
  483.4 0.0 reduce-scatter.5.cloned.1.call-update
  483.4 0.6 copy.26
  484.1 64.2 %reduce-scatter.5.cloned.1.call-done = f32[256,32]{0,1:T(8,128)} async-done(((f32[256,256]{0,1:T(8,128)}), f32[256,32]{0,1:T(8,128)}) %reduce-scatter.5.cloned.1.call-update) | async-done | bytes 32784 | tf_op jit(solution)/shard_map/reduce_scatter | solution.py:56
  548.3 5.6 %all_gather.3 = f32[1024,32]{0,1:T(8,128)S(1)} all-gather(f32[256,32]{0,1:T(8,128)} %reduce-scatter.5.cloned.1.call-done), channel_id=1, replica_groups=mesh['layer'=4,'proc'=8] {'layer'}, dimensions={0}, use_global_device_ids=true | all-gather | bytes 163840 | tf_op jit(solution)/shard_map/all_gather | solution.py:57
  553.9 0.0 copy-done
  553.9 0.2 convolution_bitcast_fusion.6
  554.2 0.7 copy.27
  (19 shorter events, 0.1 us)
Async XLA Ops:
  7.2 546.8 %copy-start = (bf16[1024,256]{1,0:T(8,128)(2,1)S(1)}, bf16[1024,256]{1,0:T(8,128)(2,1)}, u32[]{:S(2)}) copy-start(bf16[1024,256]{1,0:T(8,128)(2,1)} %param.17) | copy-start | bytes 1572868
  7.2 77.1 %all-reduce.7.cloned.1.call-start = ((), (), s32[]{:S(2)}) async-start(), calls=%async_computation.2 | async-start | bytes 262144 | tf_op jit(solution)/shard_map/psum | solution.py:9
  11.5 146.0 %all-reduce.9.cloned.1.call-start = ((), (), s32[]{:S(2)}) async-start(), calls=%async_computation.3 | async-start | bytes 262144 | tf_op jit(solution)/shard_map/psum | solution.py:9
  24.6 10.9 %copy-start.5 = (s32[1,80]{1,0:T(1,128)S(1)}, s32[1,80]{1,0:T(1,128)}, u32[]{:S(2)}) copy-start(s32[1,80]{1,0:T(1,128)} %param.14) | copy-start | bytes 964
  24.6 10.9 %copy-start.6 = (s32[1,80]{1,0:T(1,128)S(1)}, s32[1,80]{1,0:T(1,128)}, u32[]{:S(2)}) copy-start(s32[1,80]{1,0:T(1,128)} %param.15) | copy-start | bytes 964
  35.5 48.8 %copy-start.1 = (bf16[256,256]{1,0:T(8,128)(2,1)S(1)}, bf16[256,256]{1,0:T(8,128)(2,1)}, u32[]{:S(2)}) copy-start(bf16[256,256]{1,0:T(8,128)(2,1)} %param.12) | copy-start | bytes 393220
  35.5 48.8 %copy-start.2 = (bf16[256,256]{1,0:T(8,128)(2,1)S(1)}, bf16[256,256]{1,0:T(8,128)(2,1)}, u32[]{:S(2)}) copy-start(bf16[256,256]{1,0:T(8,128)(2,1)} %param.11) | copy-start | bytes 393220
  35.5 48.8 %copy-start.3 = (bf16[256,256]{1,0:T(8,128)(2,1)S(1)}, bf16[256,256]{1,0:T(8,128)(2,1)}, u32[]{:S(2)}) copy-start(bf16[256,256]{1,0:T(8,128)(2,1)} %param.10) | copy-start | bytes 393220
  49.1 504.8 %copy-start.4 = (f32[1024,32]{0,1:T(8,128)S(1)}, f32[1024,32]{0,1:T(8,128)}, u32[]{:S(2)}) copy-start(f32[1024,32]{0,1:T(8,128)} %param.16) | copy-start | bytes 393220
  86.4 144.0 %all-reduce.11.cloned.1.call-start = ((), (), s32[]{:S(2)}) async-start(), calls=%async_computation.4 | async-start | bytes 262144 | tf_op jit(solution)/shard_map/psum | solution.py:9
  159.6 143.8 %all-reduce.13.cloned.1.call-start = ((), (), s32[]{:S(2)}) async-start(), calls=%async_computation.5 | async-start | bytes 262144 | tf_op jit(solution)/shard_map/psum | solution.py:9
  232.4 143.7 %all-reduce.15.cloned.1.call-start = ((), (), s32[]{:S(2)}) async-start(), calls=%async_computation.6 | async-start | bytes 262144 | tf_op jit(solution)/shard_map/psum | solution.py:9
  305.4 143.7 %all-reduce.17.cloned.1.call-start = ((), (), s32[]{:S(2)}) async-start(), calls=%async_computation.7 | async-start | bytes 262144 | tf_op jit(solution)/shard_map/psum | solution.py:9
  378.1 105.2 %reduce-scatter.3.cloned.1.call-start = ((), (), s32[]{:S(2)}) async-start(), calls=%async_computation.8 | async-start | bytes 1310720 | tf_op jit(solution)/shard_map/reduce_scatter | solution.py:55
  459.1 89.2 %reduce-scatter.5.cloned.1.call-start = ((), (), s32[]{:S(2)}) async-start(), calls=%async_computation.9 | async-start | bytes 294912 | tf_op jit(solution)/shard_map/reduce_scatter | solution.py:56
Sparse Core Ops, SparseCore 0:
  11.9 72.3 all-reduce.6
  88.6 68.8 all-reduce.8
  161.4 68.8 all-reduce.10
  234.5 68.8 all-reduce.12
  307.2 68.8 all-reduce.14
  380.2 68.8 all-reduce.16
  459.2 24.1 reduce-scatter.2
  487.1 61.1 reduce-scatter.4
where the time goes:
time: 562 us
  waiting for transfers between devices  470 us (84%)
  matrix products  33.7 us (6%)
  local copies, waits for them, and re-layouts  33.6 us (6%)
  between operations  18 us (3%)
  blocking collectives  5.62 us (1%)
    psum x6, waiting for transfers between devices, broadcast(): return lax.psum(block, axis)  382 us
    reduce_scatter x1, waiting for transfers between devices, per_device(): lax.psum_scatter(share_sum, 'proc', scatter_dimension=1, tiled=True)  64.2 us
    reduce_scatter x1, waiting for transfers between devices, per_device(): lax.psum_scatter(partial_value, 'layer', scatter_dimension=0, tiled=True)  24.3 us
    unnamed x21, local copies, waits for them, and re-layouts  15.5 us
    dot_general x1, matrix products, per_device(): jnp.dot(pair_hot.T, factor_blocks.reshape(factor_count, block_size * bloc...  13.5 us
    reshape x1, local copies, waits for them, and re-layouts, per_device(): factor_blocks.reshape(factor_count, block_size * block_size)  13 us
    dot_general x6, matrix products, per_device(): jnp.dot(diag_inverse, reduced.astype(jnp.bfloat16), preferred_element_typ...  12.2 us
  transfers between devices with their start and end apart: 8, of which 8 were waited for; matrix products, arithmetic and copies ran while one was open for 8% of the time, Pallas kernels for 0%

commit v1 on v0

v1 whole, which is shorter than its diff:
```python
import functools

import jax
import jax.numpy as jnp
from jax import lax
from jax.experimental import pallas as pl
from jax.experimental.pallas import tpu as pltpu
from jax.sharding import PartitionSpec as P

BF16 = jnp.bfloat16
F32 = jnp.float32
VMEM_LIMIT = 24 * 1024 * 1024
SMALL_LIMIT = 8 * 1024 * 1024
OPERATOR_LIMIT = 60 * 1024 * 1024
GROUP_LIMIT = 50 * 1024 * 1024


def vmem_spec():
    return pl.BlockSpec(memory_space=pltpu.VMEM)


def smem_spec():
    return pl.BlockSpec(memory_space=pltpu.SMEM)


def operator_kernel(diag_ref, chain_ref, rhs_ref, out_ref, diag, chain, rhs, arrived):
    copies = [
        pltpu.make_async_copy(source, target, arrived.at[i])
        for i, (source, target) in enumerate([(diag_ref, diag), (chain_ref, chain), (rhs_ref, rhs)])
    ]
    for copy in copies:
        copy.start()
    for copy in copies:
        copy.wait()
    block = chain.shape[1]
    out_ref[:block, :] = (-jnp.dot(diag[...], chain[...], preferred_element_type=F32)).T.astype(BF16)
    out_ref[block:, :] = jnp.dot(diag[...], rhs[...], preferred_element_type=F32).T.astype(BF16)


def operators(diag_inverse, chain_blocks, rhs_blocks):
    block = chain_blocks.shape[0]
    inputs = (diag_inverse, chain_blocks, rhs_blocks)
    return pl.pallas_call(
        operator_kernel,
        out_shape=jax.ShapeDtypeStruct((block + rhs_blocks.shape[1], block), BF16),
        in_specs=[pl.BlockSpec(memory_space=pl.ANY)] * 3,
        out_specs=vmem_spec(),
        scratch_shapes=[pltpu.VMEM(i.shape, BF16) for i in inputs] + [pltpu.SemaphoreType.DMA((3,))],
        compiler_params=pltpu.CompilerParams(vmem_limit_bytes=OPERATOR_LIMIT),
        name="operators",
    )(*inputs)


def group_kernel(ticks, anc_count, pair_ref, factor_ref, out_ref, total, held, arrived):
    block = total.shape[1]
    chunks = arrived.shape[0]
    per_chunk = held.shape[0] // (chunks * block)

    def fetch(i):
        rows = pl.ds(pl.multiple_of(i * per_chunk * block, block), per_chunk * block)
        return pltpu.make_async_copy(factor_ref.at[rows], held.at[rows], arrived.at[i])

    for i in range(chunks):
        fetch(i).start()
    total[...] = jnp.zeros_like(total)

    def add(i, carry):
        fetch(i).wait()
        for j in range(per_chunk):
            k = i * per_chunk + j
            total[pair_ref[k]] += held[pl.ds(pl.multiple_of(k * block, block), block), :].astype(F32)
        return carry

    lax.fori_loop(0, chunks, add, 0)
    for a in range(anc_count):
        for t in range(ticks):
            out_ref[t * block : (t + 1) * block, a * block : (a + 1) * block] = total[a * ticks + t].T.astype(BF16)


def grouped(pair, factor_blocks, ticks, anc_count):
    count = pair.shape[0]
    block = factor_blocks.shape[1]
    chunks = next(count // s for s in (8, 5, 4, 2, 1) if count % s == 0)
    return pl.pallas_call(
        functools.partial(group_kernel, ticks, anc_count),
        out_shape=jax.ShapeDtypeStruct((ticks * block, anc_count * block), BF16),
        in_specs=[smem_spec(), pl.BlockSpec(memory_space=pl.ANY)],
        out_specs=vmem_spec(),
        scratch_shapes=[
            pltpu.VMEM((anc_count * ticks, block, block), F32),
            pltpu.VMEM(factor_blocks.shape, BF16),
            pltpu.SemaphoreType.DMA((chunks,)),
        ],
        compiler_params=pltpu.CompilerParams(vmem_limit_bytes=GROUP_LIMIT),
        cost_estimate=pl.CostEstimate(flops=factor_blocks.size, bytes_accessed=2 * factor_blocks.size, transcendentals=0),
        name="grouped",
    )(pair, factor_blocks)


def solve_kernel(ticks, owner_ref, group_ref, *refs):
    operator_refs, (x_ref, send_ref, keep_ref, product) = refs[:-4], refs[-4:]
    proc, core = lax.axis_index("proc"), lax.axis_index("layer") % 2
    block = operator_refs[0].shape[1]
    half = send_ref.shape[1]
    places = [(ref.at[:block], ref.at[block:]) for ref in operator_refs]
    for j, (step_ref, start_ref) in enumerate(places):

        @pl.when(owner_ref[0, 0] ^ proc == j)
        def _(start_ref=start_ref):
            x_ref[:, :block] = start_ref[...]

    def tick(t, carry):
        before = pl.multiple_of((t - 1) * block, block)
        here = pl.multiple_of(t * block, block)
        previous = x_ref[:, pl.ds(before, block)]
        for j, (step_ref, start_ref) in enumerate(places):

            @pl.when(owner_ref[0, t] ^ proc == j)
            def _(step_ref=step_ref, start_ref=start_ref):
                value = start_ref[...].astype(F32) + jnp.dot(previous, step_ref[...], preferred_element_type=F32)
                x_ref[:, pl.ds(here, block)] = value.astype(BF16)

        return carry

    lax.fori_loop(1, ticks, tick, 0)
    product[...] = jnp.dot(x_ref[...], group_ref[...], preferred_element_type=F32)
    mine = pl.multiple_of(core * half, half)
    other = pl.multiple_of((1 - core) * half, half)
    keep_ref[...] = product[:, pl.ds(mine, half)]
    send_ref[...] = product[:, pl.ds(other, half)].astype(BF16)


def solve(owner, held, group):
    ticks = owner.shape[1]
    block = held[0].shape[1]
    rhs_width = held[0].shape[0] - block
    anc_rows = group.shape[1]
    return pl.pallas_call(
        functools.partial(solve_kernel, ticks),
        out_shape=(
            jax.ShapeDtypeStruct((rhs_width, ticks * block), BF16),
            jax.ShapeDtypeStruct((rhs_width, anc_rows // 2), BF16),
            jax.ShapeDtypeStruct((rhs_width, anc_rows // 2), F32),
        ),
        in_specs=[smem_spec()] + [vmem_spec()] * (1 + len(held)),
        out_specs=(vmem_spec(), vmem_spec(), vmem_spec()),
        scratch_shapes=[pltpu.VMEM((rhs_width, anc_rows), F32)],
        compiler_params=pltpu.CompilerParams(vmem_limit_bytes=VMEM_LIMIT),
        name="solve",
    )(owner, group, *held)


def ancestor_kernel(mine_ref, other_ref, inverse_ref, out_ref):
    block = inverse_ref.shape[1]
    half = mine_ref.shape[1]
    first = lax.axis_index("layer") % 2 == 0
    mine, other = mine_ref[...], other_ref[...]
    low, high = jnp.where(first, mine, other), jnp.where(first, other, mine)
    for a in range(inverse_ref.shape[0] // block):
        rows = slice(a * block, (a + 1) * block)
        part = low if a * block < half else high
        start = a * block % half
        out_ref[:, rows] = lax.dot_general(
            part[:, start : start + block], inverse_ref[rows, :], (((1,), (1,)), ((), ())), preferred_element_type=F32
        )


def solve_ancestor(mine, other, inverse):
    return pl.pallas_call(
        ancestor_kernel,
        out_shape=jax.ShapeDtypeStruct((mine.shape[0], inverse.shape[0]), F32),
        in_specs=[vmem_spec()] * 3,
        out_specs=vmem_spec(),
        compiler_params=pltpu.CompilerParams(vmem_limit_bytes=SMALL_LIMIT),
        name="ancestor",
    )(mine, other, inverse)


def exchange(value, axis, size, mask):
    return lax.ppermute(value, axis, [(i, i ^ mask) for i in range(size)])


def gather_plan(size):
    far, mirror = size // 2, size - 2
    wanted = [(mirror, 0), (1, 0), (2, 0), (3, 2), (mirror + 1, mirror), (far, mirror), (far + 1, 1)]
    plan, held = [], {0}
    for mask, parent in wanted:
        if 0 < mask < size and mask not in held and parent in held:
            plan.append((mask, parent))
            held.add(mask)
    while len(held) < size:
        for mask in range(1, size):
            parents = [mask ^ (1 << k) for k in range(size.bit_length() - 1) if mask ^ (1 << k) in held]
            if mask not in held and parents:
                plan.append((mask, parents[0]))
                held.add(mask)
    return plan


def gathered(value, size):
    held = {0: value}
    for mask, parent in gather_plan(size):
        held[mask] = exchange(held[parent], "proc", size, mask ^ parent)
    return [held[m] for m in range(size)]


def per_device(
    layers,
    procs,
    owner,
    rhs_blocks,
    chain_blocks,
    diag_inverse,
    factor_blocks,
    col_index,
    row_index,
    anc_rhs,
    anc_inverse,
):
    ticks = owner.shape[1]
    block = chain_blocks.shape[1]
    anc_rows = anc_inverse.shape[0]
    columns = anc_rhs.shape[1]
    half = anc_rows // 2
    proc, layer = lax.axis_index("proc"), lax.axis_index("layer")

    held = gathered(operators(diag_inverse, chain_blocks, rhs_blocks), procs)
    group = grouped(row_index[0] * ticks + col_index[0], factor_blocks, ticks, anc_rows // block)
    solved_t, send, keep = solve(owner, held, group)

    total = (keep + exchange(send, "layer", layers, 1).astype(F32)).astype(BF16)
    parts = lax.all_to_all(total, "proc", 0, 0, tiled=True)
    solved_t, parts = lax.optimization_barrier((solved_t, parts))
    total = jnp.sum(parts.reshape(procs, columns, half).astype(F32), axis=0)
    for k in range(1, layers.bit_length() - 1):
        total = total + exchange(total, "layer", layers, 1 << k)
    anc_t = lax.dynamic_slice_in_dim(anc_rhs, layer % 2 * half, half, 0).T
    mine = (anc_t - total).astype(BF16)
    ancestor = solve_ancestor(mine, exchange(mine, "layer", layers, 1), anc_inverse).T
    solved = lax.dynamic_slice_in_dim(solved_t, proc * columns, columns, 0).T
    return solved, ancestor


def solution(mesh):
    placed = (
        P("layer", None),
        P(("layer", "proc"), None),
        P(("layer", "proc"), None),
        P(("layer", "proc"), None),
        P(("layer", "proc"), None),
        P(("layer", "proc"), None),
        P(("layer", "proc"), None),
        P(None, "proc"),
        P(),
    )
    return jax.shard_map(
        functools.partial(per_device, mesh.shape["layer"], mesh.shape["proc"]),
        mesh=mesh,
        in_specs=placed,
        out_specs=(P("layer", "proc"), P(None, "proc")),
        check_vma=False,
    )
```

time: 562 us -> 59.8 us (0.11)
  waiting for transfers between devices: 470 us -> 17.6 us
  matrix products: 33.7 us -> 0 us
  local copies, waits for them, and re-layouts: 33.6 us -> 0.68 us
  between operations: 18 us -> 0.73 us
  starting transfers between devices: 0.51 us -> 15.8 us
  Pallas kernels: 0 us -> 11.8 us
  blocking collectives: 5.62 us -> 12.3 us
    psum x6 -> x0, waiting for transfers between devices: 382 us -> none  [broadcast(): return lax.psum(block, axis)]
    reduce_scatter x2 -> x0, waiting for transfers between devices: 88.5 us -> none  [the longest x1 64.2 us: per_device(): lax.psum_scatter(share_sum, 'proc', scatter_dimension=1, tiled=True)]
    dot_general x9 -> x0, matrix products: 33.7 us -> none  [the longest x1 13.5 us: per_device(): jnp.dot(pair_hot.T, factor_blocks.reshape(factor_count, block_size * bloc...]
    ppermute x0 -> x10, waiting for transfers between devices: none -> 17.6 us  [exchange(): return lax.ppermute(value, axis, [(i, i ^ mask) for i in range(size)])]
    ppermute x0 -> x10, starting transfers between devices: none -> 15.8 us  [exchange(): return lax.ppermute(value, axis, [(i, i ^ mask) for i in range(size)])]
    reshape x4 -> x0, local copies, waits for them, and re-layouts: 15.7 us -> none  [the longest x1 13 us: per_device(): factor_blocks.reshape(factor_count, block_size * block_size)]
    unnamed x21 -> x8, local copies, waits for them, and re-layouts: 15.5 us -> 0.02 us
    all_to_all x0 -> x1, blocking collectives: none -> 12.3 us  [per_device(): parts = lax.all_to_all(total, 'proc', 0, 0, tiled=True)]
  transfers between devices with their start and end apart: 8 -> 10, of which waited for: 8 -> 6; matrix products, arithmetic and copies ran while one was open for 8% -> 2% of each run, Pallas kernels for 0% -> 10%
where the time goes in v1:
time: 59.8 us; the launch traced here: 59.7 us
  waiting for transfers between devices  17.6 us (29%)
  starting transfers between devices  15.8 us (26%)
  blocking collectives  12.3 us (21%)
  Pallas kernels  11.8 us (20%)
  other arithmetic  0.81 us (1%)
  between operations  0.73 us (1%)
  local copies, waits for them, and re-layouts  0.68 us (1%)
    ppermute x10, waiting for transfers between devices, exchange(): return lax.ppermute(value, axis, [(i, i ^ mask) for i in range(size)])  17.6 us
    ppermute x10, starting transfers between devices, exchange(): return lax.ppermute(value, axis, [(i, i ^ mask) for i in range(size)])  15.8 us
    all_to_all x1, blocking collectives, per_device(): parts = lax.all_to_all(total, 'proc', 0, 0, tiled=True)  12.3 us
    pallas_call x1, Pallas kernels, grouped(): pl.pallas_call(functools.partial(group_kernel, ticks, anc_count), out_sha...  5.75 us
    pallas_call x1, Pallas kernels, solve(): pl.pallas_call(functools.partial(solve_kernel, ticks), out_shape=(jax.Sha...  2.99 us
    pallas_call x1, Pallas kernels, operators(): pl.pallas_call(operator_kernel, out_shape=jax.ShapeDtypeStruct((block + r...  2.1 us
  transfers between devices with their start and end apart: 10, of which 6 were waited for; matrix products, arithmetic and copies ran while one was open for 2% of the time, Pallas kernels for 10%

profile of v1, /device:TPU:0, one launch (start us, length us, event | category | flops | bytes accessed | tf_op | source)
XLA Modules:
  0.0 59.7 jit_solution(13366374959082982189)
XLA Ops:
  0.6 0.0 copy-start.2
  0.6 2.1 %operators.1.refs_0_ = bf16[512,256]{1,0:T(8,128)(2,1)} custom-call(bf16[256,256]{1,0:T(8,128)(2,1)} %diag_ref.1, bf16[256,256]{1,0:T(8,128)(2,1)} %chain_ref.1, bf16[256,256]{1,0:T(8,128)(2,1)} %rhs_ref.1), custom_call_target="tpu_custom_call" | custom-call | tf_op jit(solution)/shard_map/operators/pallas_call | solution.py:43
  2.7 0.0 copy-start
  2.8 0.0 copy-start.3
  2.8 5.1 %collective-permute-start.3 = (bf16[512,256]{1,0:T(8,128)(2,1)}, bf16[512,256]{1,0:T(8,128)(2,1)S(1)}, u32[]{:S(2)}, u32[]{:S(2)}) collective-permute-start(bf16[512,256]{1,0:T(8,128)(2,1)} %operators.1.refs_0_), channel_id=1, source_target_pairs={{0,6},{1,7},{2,4},{3,5},{4,2},{5,3},{6,0},{7,1},{8,14},{9,15},{10,... | collective-permute-start | bytes 786440 | tf_op jit(solution)/shard_map/ppermute | solution.py:180
  7.9 0.0 collective-permute-start.1
  7.9 1.5 %collective-permute-start = (bf16[512,256]{1,0:T(8,128)(2,1)}, bf16[512,256]{1,0:T(8,128)(2,1)S(1)}, u32[]{:S(2)}, u32[]{:S(2)}) collective-permute-start(bf16[512,256]{1,0:T(8,128)(2,1)} %operators.1.refs_0_), channel_id=1, source_target_pairs={{0,1},{1,0},{2,3},{3,2},{4,5},{5,4},{6,7},{7,6},{8,9},{9,8},{10,11... | collective-permute-start | bytes 786440 | tf_op jit(solution)/shard_map/ppermute | solution.py:180
  9.4 5.9 %collective-permute-done.3.refs_6_ = bf16[512,256]{1,0:T(8,128)(2,1)S(1)} collective-permute-done((bf16[512,256]{1,0:T(8,128)(2,1)}, bf16[512,256]{1,0:T(8,128)(2,1)S(1)}, u32[]{:S(2)}, u32[]{:S(2)}) %collective-permute-start.3) | collective-permute-done | bytes 262176 | tf_op jit(solution)/shard_map/ppermute | solution.py:180
  15.3 4.4 %collective-permute-start.4 = (bf16[512,256]{1,0:T(8,128)(2,1)S(1)}, bf16[512,256]{1,0:T(8,128)(2,1)S(1)}, u32[]{:S(2)}, u32[]{:S(2)}) collective-permute-start(bf16[512,256]{1,0:T(8,128)(2,1)S(1)} %collective-permute-done.3.refs_6_), channel_id=1, source_target_pairs={{0,2},{1,3},{2,0},{3,1},{4,6},{5,7},{6,4},{7,5},{8,10},{9,11},{10,... | collective-permute-start | bytes 786440 | tf_op jit(solution)/shard_map/ppermute | solution.py:180
  19.7 1.5 %collective-permute-start.6 = (bf16[512,256]{1,0:T(8,128)(2,1)S(1)}, bf16[512,256]{1,0:T(8,128)(2,1)S(1)}, u32[]{:S(2)}, u32[]{:S(2)}) collective-permute-start(bf16[512,256]{1,0:T(8,128)(2,1)S(1)} %collective-permute-done.3.refs_6_), channel_id=1, source_target_pairs={{0,1},{1,0},{2,3},{3,2},{4,5},{5,4},{6,7},{7,6},{8,9},{9,8},{10,11... | collective-permute-start | bytes 786440 | tf_op jit(solution)/shard_map/ppermute | solution.py:180
  21.3 0.0 collective-permute-done.1.refs_2_
  21.3 0.5 collective-permute-start.2
  21.8 0.0 collective-permute-done.refs_1_
  21.8 1.0 %collective-permute-start.5 = (bf16[512,256]{1,0:T(8,128)(2,1)S(1)}, bf16[512,256]{1,0:T(8,128)(2,1)S(1)}, u32[]{:S(2)}, u32[]{:S(2)}) collective-permute-start(bf16[512,256]{1,0:T(8,128)(2,1)S(1)} %collective-permute-done.refs_1_), channel_id=1, source_target_pairs={{0,4},{1,5},{2,6},{3,7},{4,0},{5,1},{6,2},{7,3},{8,12},{9,13},{10,... | collective-permute-start | bytes 786440 | tf_op jit(solution)/shard_map/ppermute | solution.py:180
  22.8 0.7 %add_bitcast_fusion.pair_ref = s32[80]{0:T(128)S(1)} fusion(s32[1,80]{1,0:T(1,128)} %param.14, s32[1,80]{1,0:T(1,128)} %param.15), kind=kLoop, calls=%fused_computation.5 | loop fusion | flops 160 | bytes 960 | tf_op jit(solution)/shard_map/add | solution.py:228
  23.5 0.0 copy-start.1
  23.5 5.8 %grouped.1.group_ref = bf16[1536,1024]{1,0:T(8,128)(2,1)S(1)} custom-call(s32[80]{0:T(128)S(1)} %add_bitcast_fusion.pair_ref, bf16[20480,256]{1,0:T(8,128)(2,1)} %factor_ref.1), custom_call_target="tpu_custom_call" | custom-call | flops 5242880 | bytes 10485760 | tf_op jit(solution)/shard_map/grouped/pallas_call | solution.py:84
  29.2 0.0 collective-permute-done.4.refs_4_
  29.2 0.0 collective-permute-done.6.refs_7_
  29.2 3.2 %collective-permute-done.2.refs_3_ = bf16[512,256]{1,0:T(8,128)(2,1)S(1)} collective-permute-done((bf16[512,256]{1,0:T(8,128)(2,1)S(1)}, bf16[512,256]{1,0:T(8,128)(2,1)S(1)}, u32[]{:S(2)}, u32[]{:S(2)}) %collective-permute-start.2) | collective-permute-done | bytes 262176 | tf_op jit(solution)/shard_map/ppermute | solution.py:180
  32.4 3.7 %collective-permute-done.5.refs_5_ = bf16[512,256]{1,0:T(8,128)(2,1)S(1)} collective-permute-done((bf16[512,256]{1,0:T(8,128)(2,1)S(1)}, bf16[512,256]{1,0:T(8,128)(2,1)S(1)}, u32[]{:S(2)}, u32[]{:S(2)}) %collective-permute-start.5) | collective-permute-done | bytes 262176 | tf_op jit(solution)/shard_map/ppermute | solution.py:180
  36.1 0.0 copy-done.2
  36.1 0.0 copy-done
  36.1 3.0 %solve.1 = (bf16[256,1536]{1,0:T(8,128)(2,1)S(1)}, bf16[256,512]{1,0:T(8,128)(2,1)S(1)}, f32[256,512]{1,0:T(8,128)S(1)}) custom-call(s32[1,6]{1,0:T(1,128)S(1)} %copy-done.2, bf16[1536,1024]{1,0:T(8,128)(2,1)S(1)} %grouped.1.group_ref, bf16[512,256]{1,0:T(8,128)(2,1)S(1)} %copy-done, bf16[512,256]{1,0:T(8,128)(2,1)S(1)} %collective-permute-done.refs_1_, ...), custom_call_target="tpu_custom_call" | custom-call | tf_op jit(solution)/shard_map/solve/pallas_call | solution.py:138
  39.1 0.1 collective-permute-start.7
  39.2 1.5 %collective-permute-done.7 = bf16[256,512]{1,0:T(8,128)(2,1)S(1)} collective-permute-done((bf16[256,512]{1,0:T(8,128)(2,1)S(1)}, bf16[256,512]{1,0:T(8,128)(2,1)S(1)}, u32[]{:S(2)}, u32[]{:S(2)}) %collective-permute-start.7) | collective-permute-done | bytes 262176 | tf_op jit(solution)/shard_map/ppermute | solution.py:180
  40.7 0.1 add_convert_fusion
  40.8 12.3 %all_to_all.12 = bf16[8,32,512]{2,1,0:T(8,128)(2,1)S(1)} all-to-all(bf16[8,32,512]{2,1,0:T(8,128)(2,1)S(1)} %bitcast.13), channel_id=1, replica_groups=mesh['layer'=4,'proc'=8] {'proc'}, dimensions={0} | all-to-all | bytes 524288 | tf_op jit(solution)/shard_map/all_to_all | solution.py:232
  53.1 1.6 %collective-permute-start.8 = (f32[32,512]{1,0:T(8,128)S(1)}, f32[32,512]{1,0:T(8,128)S(1)}, u32[]{:S(2)}, u32[]{:S(2)}) collective-permute-start(f32[32,512]{1,0:T(8,128)S(1)} %convert_reduce_fusion), channel_id=1, source_target_pairs={{0,16},{8,24},{16,0},{24,8},{1,17},{9,25},{17,1},{25,9},{2,18},{10... | collective-permute-start | bytes 196616 | tf_op jit(solution)/shard_map/ppermute | solution.py:180
  54.7 2.8 %collective-permute-done.8 = f32[32,512]{1,0:T(8,128)S(1)} collective-permute-done((f32[32,512]{1,0:T(8,128)S(1)}, f32[32,512]{1,0:T(8,128)S(1)}, u32[]{:S(2)}, u32[]{:S(2)}) %collective-permute-start.8) | collective-permute-done | bytes 65568 | tf_op jit(solution)/shard_map/ppermute | solution.py:180
  57.4 0.0 copy-done.3
  57.5 0.1 collective-permute-start.9
  57.6 0.7 %dynamic-slice_bitcast_fusion = bf16[1536,32]{0,1:T(8,128)(2,1)} fusion(bf16[256,1536]{1,0:T(8,128)(2,1)S(1)} %get-tuple-element.10, s32[]{:T(128)S(6)} %select_n.13), kind=kLoop, calls=%fused_computation.2 | loop fusion | bytes 196612 | tf_op jit(solution)/shard_map/transpose | solution.py:240
  58.2 0.5 collective-permute-done.9.other_ref
  58.7 0.0 copy-done.1
  58.7 0.9 %ancestor.1 = f32[32,1024]{1,0:T(8,128)} custom-call(bf16[32,512]{1,0:T(8,128)(2,1)S(1)} %fusion.mine_ref, bf16[32,512]{1,0:T(8,128)(2,1)S(1)} %collective-permute-done.9.other_ref, bf16[1024,256]{1,0:T(8,128)(2,1)S(1)} %copy-done.1), custom_call_target="tpu_custom_call" | custom-call | tf_op jit(solution)/shard_map/ancestor/pallas_call | solution.py:169
  (2 shorter events, 0.1 us)
Async XLA Ops:
  0.6 35.5 %copy-start.2 = (s32[1,6]{1,0:T(1,128)S(1)}, s32[1,6]{1,0:T(1,128)}, u32[]{:S(2)}) copy-start(s32[1,6]{1,0:T(1,128)} %owner_ref.1) | copy-start | bytes 76
  2.7 33.4 %copy-start = (bf16[512,256]{1,0:T(8,128)(2,1)S(1)}, bf16[512,256]{1,0:T(8,128)(2,1)}, u32[]{:S(2)}) copy-start(bf16[512,256]{1,0:T(8,128)(2,1)} %operators.1.refs_0_) | copy-start | bytes 786436
  2.8 54.7 %copy-start.3 = (f32[1024,32]{0,1:T(8,128)S(1)}, f32[1024,32]{0,1:T(8,128)}, u32[]{:S(2)}) copy-start(f32[1024,32]{0,1:T(8,128)} %param.16) | copy-start | bytes 393220
  2.8 12.5 %collective-permute-start.3 = (bf16[512,256]{1,0:T(8,128)(2,1)}, bf16[512,256]{1,0:T(8,128)(2,1)S(1)}, u32[]{:S(2)}, u32[]{:S(2)}) collective-permute-start(bf16[512,256]{1,0:T(8,128)(2,1)} %operators.1.refs_0_), channel_id=1, source_target_pairs={{0,6},{1,7},{2,4},{3,5},{4,2},{5,3},{6,0},{7,1},{8,14},{9,15},{10,... | collective-permute-start | bytes 786440 | tf_op jit(solution)/shard_map/ppermute | solution.py:180
  7.9 13.4 %collective-permute-start.1 = (bf16[512,256]{1,0:T(8,128)(2,1)}, bf16[512,256]{1,0:T(8,128)(2,1)S(1)}, u32[]{:S(2)}, u32[]{:S(2)}) collective-permute-start(bf16[512,256]{1,0:T(8,128)(2,1)} %operators.1.refs_0_), channel_id=1, source_target_pairs={{0,2},{1,3},{2,0},{3,1},{4,6},{5,7},{6,4},{7,5},{8,10},{9,11},{10,... | collective-permute-start | bytes 786440 | tf_op jit(solution)/shard_map/ppermute | solution.py:180
  7.9 13.9 %collective-permute-start = (bf16[512,256]{1,0:T(8,128)(2,1)}, bf16[512,256]{1,0:T(8,128)(2,1)S(1)}, u32[]{:S(2)}, u32[]{:S(2)}) collective-permute-start(bf16[512,256]{1,0:T(8,128)(2,1)} %operators.1.refs_0_), channel_id=1, source_target_pairs={{0,1},{1,0},{2,3},{3,2},{4,5},{5,4},{6,7},{7,6},{8,9},{9,8},{10,11... | collective-permute-start | bytes 786440 | tf_op jit(solution)/shard_map/ppermute | solution.py:180
  15.3 13.9 %collective-permute-start.4 = (bf16[512,256]{1,0:T(8,128)(2,1)S(1)}, bf16[512,256]{1,0:T(8,128)(2,1)S(1)}, u32[]{:S(2)}, u32[]{:S(2)}) collective-permute-start(bf16[512,256]{1,0:T(8,128)(2,1)S(1)} %collective-permute-done.3.refs_6_), channel_id=1, source_target_pairs={{0,2},{1,3},{2,0},{3,1},{4,6},{5,7},{6,4},{7,5},{8,10},{9,11},{10,... | collective-permute-start | bytes 786440 | tf_op jit(solution)/shard_map/ppermute | solution.py:180
  19.7 9.5 %collective-permute-start.6 = (bf16[512,256]{1,0:T(8,128)(2,1)S(1)}, bf16[512,256]{1,0:T(8,128)(2,1)S(1)}, u32[]{:S(2)}, u32[]{:S(2)}) collective-permute-start(bf16[512,256]{1,0:T(8,128)(2,1)S(1)} %collective-permute-done.3.refs_6_), channel_id=1, source_target_pairs={{0,1},{1,0},{2,3},{3,2},{4,5},{5,4},{6,7},{7,6},{8,9},{9,8},{10,11... | collective-permute-start | bytes 786440 | tf_op jit(solution)/shard_map/ppermute | solution.py:180
  21.3 11.2 %collective-permute-start.2 = (bf16[512,256]{1,0:T(8,128)(2,1)S(1)}, bf16[512,256]{1,0:T(8,128)(2,1)S(1)}, u32[]{:S(2)}, u32[]{:S(2)}) collective-permute-start(bf16[512,256]{1,0:T(8,128)(2,1)S(1)} %collective-permute-done.1.refs_2_), channel_id=1, source_target_pairs={{0,1},{1,0},{2,3},{3,2},{4,5},{5,4},{6,7},{7,6},{8,9},{9,8},{10,11... | collective-permute-start | bytes 786440 | tf_op jit(solution)/shard_map/ppermute | solution.py:180
  21.8 14.4 %collective-permute-start.5 = (bf16[512,256]{1,0:T(8,128)(2,1)S(1)}, bf16[512,256]{1,0:T(8,128)(2,1)S(1)}, u32[]{:S(2)}, u32[]{:S(2)}) collective-permute-start(bf16[512,256]{1,0:T(8,128)(2,1)S(1)} %collective-permute-done.refs_1_), channel_id=1, source_target_pairs={{0,4},{1,5},{2,6},{3,7},{4,0},{5,1},{6,2},{7,3},{8,12},{9,13},{10,... | collective-permute-start | bytes 786440 | tf_op jit(solution)/shard_map/ppermute | solution.py:180
  23.5 35.3 %copy-start.1 = (bf16[1024,256]{1,0:T(8,128)(2,1)S(1)}, bf16[1024,256]{1,0:T(8,128)(2,1)}, u32[]{:S(2)}) copy-start(bf16[1024,256]{1,0:T(8,128)(2,1)} %inverse_ref.1) | copy-start | bytes 1572868
  39.1 1.6 %collective-permute-start.7 = (bf16[256,512]{1,0:T(8,128)(2,1)S(1)}, bf16[256,512]{1,0:T(8,128)(2,1)S(1)}, u32[]{:S(2)}, u32[]{:S(2)}) collective-permute-start(bf16[256,512]{1,0:T(8,128)(2,1)S(1)} %get-tuple-element.9), channel_id=1, source_target_pairs={{0,8},{8,0},{16,24},{24,16},{1,9},{9,1},{17,25},{25,17},{2,10},{10... | collective-permute-start | bytes 786440 | tf_op jit(solution)/shard_map/ppermute | solution.py:180
  53.1 4.3 %collective-permute-start.8 = (f32[32,512]{1,0:T(8,128)S(1)}, f32[32,512]{1,0:T(8,128)S(1)}, u32[]{:S(2)}, u32[]{:S(2)}) collective-permute-start(f32[32,512]{1,0:T(8,128)S(1)} %convert_reduce_fusion), channel_id=1, source_target_pairs={{0,16},{8,24},{16,0},{24,8},{1,17},{9,25},{17,1},{25,9},{2,18},{10... | collective-permute-start | bytes 196616 | tf_op jit(solution)/shard_map/ppermute | solution.py:180
  57.5 1.3 %collective-permute-start.9 = (bf16[32,512]{1,0:T(8,128)(2,1)S(1)}, bf16[32,512]{1,0:T(8,128)(2,1)S(1)}, u32[]{:S(2)}, u32[]{:S(2)}) collective-permute-start(bf16[32,512]{1,0:T(8,128)(2,1)S(1)} %fusion.mine_ref), channel_id=1, source_target_pairs={{0,8},{8,0},{16,24},{24,16},{1,9},{9,1},{17,25},{25,17},{2,10},{10... | collective-permute-start | bytes 98312 | tf_op jit(solution)/shard_map/ppermute | solution.py:180

commit v2 on v1

--- a/solution.py
+++ b/solution.py
@@ -98,32 +98,30 @@
 
 
 def solve_kernel(ticks, owner_ref, group_ref, *refs):
-    operator_refs, (x_ref, send_ref, keep_ref, product) = refs[:-4], refs[-4:]
+    operator_refs, (x_ref, send_ref, keep_ref, product, chosen) = refs[:-5], refs[-5:]
     proc, core = lax.axis_index("proc"), lax.axis_index("layer") % 2
-    block = operator_refs[0].shape[1]
+    block = chosen.shape[2]
     half = send_ref.shape[1]
-    places = [(ref.at[:block], ref.at[block:]) for ref in operator_refs]
-    for j, (step_ref, start_ref) in enumerate(places):
-
-        @pl.when(owner_ref[0, 0] ^ proc == j)
-        def _(start_ref=start_ref):
-            x_ref[:, :block] = start_ref[...]
-
-    def tick(t, carry):
-        before = pl.multiple_of((t - 1) * block, block)
-        here = pl.multiple_of(t * block, block)
-        previous = x_ref[:, pl.ds(before, block)]
-        for j, (step_ref, start_ref) in enumerate(places):
+    for t in range(ticks):
+        for j, ref in enumerate(operator_refs):
 
             @pl.when(owner_ref[0, t] ^ proc == j)
-            def _(step_ref=step_ref, start_ref=start_ref):
-                value = start_ref[...].astype(F32) + jnp.dot(previous, step_ref[...], preferred_element_type=F32)
-                x_ref[:, pl.ds(here, block)] = value.astype(BF16)
-
-        return carry
-
-    lax.fori_loop(1, ticks, tick, 0)
-    product[...] = jnp.dot(x_ref[...], group_ref[...], preferred_element_type=F32)
+            def _(t=t, ref=ref):
+                chosen[t] = ref[...]
+
+    def update(t):
+        part = jnp.dot(x_ref[:, t * block : (t + 1) * block], group_ref[t * block : (t + 1) * block, :], preferred_element_type=F32)
+        product[...] = part if t == 0 else product[...] + part
+
+    for t in range(ticks):
+        if t == 0:
+            x_ref[:, :block] = chosen[0, block:, :]
+        else:
+            previous = x_ref[:, (t - 1) * block : t * block]
+            value = jnp.dot(previous, chosen[t, :block, :], preferred_element_type=F32)
+            x_ref[:, t * block : (t + 1) * block] = (chosen[t, block:, :].astype(F32) + value).astype(BF16)
+            update(t - 1)
+    update(ticks - 1)
     mine = pl.multiple_of(core * half, half)
     other = pl.multiple_of((1 - core) * half, half)
     keep_ref[...] = product[:, pl.ds(mine, half)]
@@ -144,7 +142,10 @@
         ),
         in_specs=[smem_spec()] + [vmem_spec()] * (1 + len(held)),
         out_specs=(vmem_spec(), vmem_spec(), vmem_spec()),
-        scratch_shapes=[pltpu.VMEM((rhs_width, anc_rows), F32)],
+        scratch_shapes=[
+            pltpu.VMEM((rhs_width, anc_rows), F32),
+            pltpu.VMEM((ticks, *held[0].shape), BF16),
+        ],
         compiler_params=pltpu.CompilerParams(vmem_limit_bytes=VMEM_LIMIT),
         name="solve",
     )(owner, group, *held)
@@ -182,7 +183,7 @@
 
 def gather_plan(size):
     far, mirror = size // 2, size - 2
-    wanted = [(mirror, 0), (1, 0), (2, 0), (3, 2), (mirror + 1, mirror), (far, mirror), (far + 1, 1)]
+    wanted = [(mirror, 0), (1, 0), (2, 0), (far + 1, 1), (3, 2), (mirror + 1, mirror), (far, mirror)]
     plan, held = [], {0}
     for mask, parent in wanted:
         if 0 < mask < size and mask not in held and parent in held:
@@ -197,11 +198,13 @@
     return plan
 
 
-def gathered(value, size):
-    held = {0: value}
+def gathered(value, size, make_group):
+    held, group = {0: value}, None
     for mask, parent in gather_plan(size):
+        if parent and group is None:
+            group, held[1] = lax.optimization_barrier((make_group(), held[1]))
         held[mask] = exchange(held[parent], "proc", size, mask ^ parent)
-    return [held[m] for m in range(size)]
+    return [held[m] for m in range(size)], make_group() if group is None else group
 
 
 def per_device(
@@ -224,8 +227,11 @@
     half = anc_rows // 2
     proc, layer = lax.axis_index("proc"), lax.axis_index("layer")
 
-    held = gathered(operators(diag_inverse, chain_blocks, rhs_blocks), procs)
-    group = grouped(row_index[0] * ticks + col_index[0], factor_blocks, ticks, anc_rows // block)
+    held, group = gathered(
+        operators(diag_inverse, chain_blocks, rhs_blocks),
+        procs,
+        lambda: grouped(row_index[0] * ticks + col_index[0], factor_blocks, ticks, anc_rows // block),
+    )
     solved_t, send, keep = solve(owner, held, group)
 
     total = (keep + exchange(send, "layer", layers, 1).astype(F32)).astype(BF16)

time: 59.8 us -> 56.7 us (0.948)
  waiting for transfers between devices: 17.6 us -> 13.5 us
  starting transfers between devices: 15.8 us -> 17.5 us
  Pallas kernels: 11.8 us -> 11.1 us
    ppermute x10, waiting for transfers between devices: 17.6 us -> 13.5 us  [exchange(): return lax.ppermute(value, axis, [(i, i ^ mask) for i in range(size)])]
    ppermute x10, starting transfers between devices: 15.8 us -> 17.5 us  [exchange(): return lax.ppermute(value, axis, [(i, i ^ mask) for i in range(size)])]
    pallas_call x1, Pallas kernels: 2.99 us -> 2.28 us  [solve(): pl.pallas_call(functools.partial(solve_kernel, ticks), out_shape=(jax.Sha...]
  transfers between devices with their start and end apart: 10 -> 10, of which waited for: 6 -> 7; matrix products, arithmetic and copies ran while one was open for 2% -> 2% of each run, Pallas kernels for 10% -> 10%
where the time goes in v2:
time: 56.7 us; the launch traced here: 56.5 us
  starting transfers between devices  17.5 us (31%)
  waiting for transfers between devices  13.5 us (24%)
  blocking collectives  12.3 us (22%)
  Pallas kernels  11.1 us (20%)
  other arithmetic  0.81 us (1%)
  between operations  0.72 us (1%)
  local copies, waits for them, and re-layouts  0.68 us (1%)
    ppermute x10, starting transfers between devices, exchange(): return lax.ppermute(value, axis, [(i, i ^ mask) for i in range(size)])  17.5 us
    ppermute x10, waiting for transfers between devices, exchange(): return lax.ppermute(value, axis, [(i, i ^ mask) for i in range(size)])  13.5 us
    all_to_all x1, blocking collectives, per_device(): parts = lax.all_to_all(total, 'proc', 0, 0, tiled=True)  12.3 us
    pallas_call x1, Pallas kernels, grouped(): pl.pallas_call(functools.partial(group_kernel, ticks, anc_count), out_sha...  5.75 us
    pallas_call x1, Pallas kernels, solve(): pl.pallas_call(functools.partial(solve_kernel, ticks), out_shape=(jax.Sha...  2.28 us
    pallas_call x1, Pallas kernels, operators(): pl.pallas_call(operator_kernel, out_shape=jax.ShapeDtypeStruct((block + r...  2.1 us
  transfers between devices with their start and end apart: 10, of which 7 were waited for; matrix products, arithmetic and copies ran while one was open for 2% of the time, Pallas kernels for 10%

profile of v2, /device:TPU:0, one launch (start us, length us, event | category | flops | bytes accessed | tf_op | source)
XLA Modules:
  0.0 56.5 jit_solution(2625705730170713742)
XLA Ops:
  0.6 0.0 copy-start.2
  0.6 2.1 %operators.1.refs_0_ = bf16[512,256]{1,0:T(8,128)(2,1)} custom-call(bf16[256,256]{1,0:T(8,128)(2,1)} %diag_ref.1, bf16[256,256]{1,0:T(8,128)(2,1)} %chain_ref.1, bf16[256,256]{1,0:T(8,128)(2,1)} %rhs_ref.1), custom_call_target="tpu_custom_call" | custom-call | tf_op jit(solution)/shard_map/operators/pallas_call | solution.py:43
  2.7 0.0 copy-start
  2.8 0.0 copy-start.3
  2.8 3.0 %collective-permute-start = (bf16[512,256]{1,0:T(8,128)(2,1)}, bf16[512,256]{1,0:T(8,128)(2,1)S(1)}, u32[]{:S(2)}, u32[]{:S(2)}) collective-permute-start(bf16[512,256]{1,0:T(8,128)(2,1)} %operators.1.refs_0_), channel_id=1, source_target_pairs={{0,1},{1,0},{2,3},{3,2},{4,5},{5,4},{6,7},{7,6},{8,9},{9,8},{10,11... | collective-permute-start | bytes 786440 | tf_op jit(solution)/shard_map/ppermute | solution.py:181
  5.8 3.6 %collective-permute-start.3 = (bf16[512,256]{1,0:T(8,128)(2,1)}, bf16[512,256]{1,0:T(8,128)(2,1)S(1)}, u32[]{:S(2)}, u32[]{:S(2)}) collective-permute-start(bf16[512,256]{1,0:T(8,128)(2,1)} %operators.1.refs_0_), channel_id=1, source_target_pairs={{0,6},{1,7},{2,4},{3,5},{4,2},{5,3},{6,0},{7,1},{8,14},{9,15},{10,... | collective-permute-start | bytes 786440 | tf_op jit(solution)/shard_map/ppermute | solution.py:181
  9.4 0.0 collective-permute-start.1
  9.4 0.7 %add_bitcast_fusion.pair_ref = s32[80]{0:T(128)S(1)} fusion(s32[1,80]{1,0:T(1,128)} %param.14, s32[1,80]{1,0:T(1,128)} %param.15), kind=kLoop, calls=%fused_computation.5 | loop fusion | flops 160 | bytes 960 | tf_op jit(solution)/shard_map/add | solution.py:233
  10.1 0.0 copy-start.1
  10.1 5.8 %grouped.1.group_ref = bf16[1536,1024]{1,0:T(8,128)(2,1)S(1)} custom-call(s32[80]{0:T(128)S(1)} %add_bitcast_fusion.pair_ref, bf16[20480,256]{1,0:T(8,128)(2,1)} %factor_ref.1), custom_call_target="tpu_custom_call" | custom-call | flops 5242880 | bytes 10485760 | tf_op jit(solution)/shard_map/grouped/pallas_call | solution.py:84
  15.8 0.0 collective-permute-done.refs_1_
  15.9 0.8 %collective-permute-start.5 = (bf16[512,256]{1,0:T(8,128)(2,1)S(1)}, bf16[512,256]{1,0:T(8,128)(2,1)S(1)}, u32[]{:S(2)}, u32[]{:S(2)}) collective-permute-start(bf16[512,256]{1,0:T(8,128)(2,1)S(1)} %collective-permute-done.refs_1_), channel_id=1, source_target_pairs={{0,4},{1,5},{2,6},{3,7},{4,0},{5,1},{6,2},{7,3},{8,12},{9,13},{10,... | collective-permute-start | bytes 786440 | tf_op jit(solution)/shard_map/ppermute | solution.py:181
  16.7 0.4 collective-permute-done.3.refs_6_
  17.1 6.3 %collective-permute-start.4 = (bf16[512,256]{1,0:T(8,128)(2,1)S(1)}, bf16[512,256]{1,0:T(8,128)(2,1)S(1)}, u32[]{:S(2)}, u32[]{:S(2)}) collective-permute-start(bf16[512,256]{1,0:T(8,128)(2,1)S(1)} %collective-permute-done.3.refs_6_), channel_id=1, source_target_pairs={{0,2},{1,3},{2,0},{3,1},{4,6},{5,7},{6,4},{7,5},{8,10},{9,11},{10,... | collective-permute-start | bytes 786440 | tf_op jit(solution)/shard_map/ppermute | solution.py:181
  23.3 0.3 collective-permute-start.6
  23.6 0.0 collective-permute-done.1.refs_2_
  23.6 1.7 %collective-permute-start.2 = (bf16[512,256]{1,0:T(8,128)(2,1)S(1)}, bf16[512,256]{1,0:T(8,128)(2,1)S(1)}, u32[]{:S(2)}, u32[]{:S(2)}) collective-permute-start(bf16[512,256]{1,0:T(8,128)(2,1)S(1)} %collective-permute-done.1.refs_2_), channel_id=1, source_target_pairs={{0,1},{1,0},{2,3},{3,2},{4,5},{5,4},{6,7},{7,6},{8,9},{9,8},{10,11... | collective-permute-start | bytes 786440 | tf_op jit(solution)/shard_map/ppermute | solution.py:181
  25.4 6.4 %collective-permute-done.5.refs_5_ = bf16[512,256]{1,0:T(8,128)(2,1)S(1)} collective-permute-done((bf16[512,256]{1,0:T(8,128)(2,1)S(1)}, bf16[512,256]{1,0:T(8,128)(2,1)S(1)}, u32[]{:S(2)}, u32[]{:S(2)}) %collective-permute-start.5) | collective-permute-done | bytes 262176 | tf_op jit(solution)/shard_map/ppermute | solution.py:181
  31.8 0.9 %collective-permute-done.4.refs_4_ = bf16[512,256]{1,0:T(8,128)(2,1)S(1)} collective-permute-done((bf16[512,256]{1,0:T(8,128)(2,1)S(1)}, bf16[512,256]{1,0:T(8,128)(2,1)S(1)}, u32[]{:S(2)}, u32[]{:S(2)}) %collective-permute-start.4) | collective-permute-done | bytes 262176 | tf_op jit(solution)/shard_map/ppermute | solution.py:181
  32.6 0.0 collective-permute-done.6.refs_7_
  32.6 1.0 %collective-permute-done.2.refs_3_ = bf16[512,256]{1,0:T(8,128)(2,1)S(1)} collective-permute-done((bf16[512,256]{1,0:T(8,128)(2,1)S(1)}, bf16[512,256]{1,0:T(8,128)(2,1)S(1)}, u32[]{:S(2)}, u32[]{:S(2)}) %collective-permute-start.2) | collective-permute-done | bytes 262176 | tf_op jit(solution)/shard_map/ppermute | solution.py:181
  33.6 0.0 copy-done.2
  33.6 0.0 copy-done
  33.6 2.3 %solve.1 = (bf16[256,1536]{1,0:T(8,128)(2,1)S(1)}, bf16[256,512]{1,0:T(8,128)(2,1)S(1)}, f32[256,512]{1,0:T(8,128)S(1)}) custom-call(s32[1,6]{1,0:T(1,128)S(1)} %copy-done.2, bf16[1536,1024]{1,0:T(8,128)(2,1)S(1)} %grouped.1.group_ref, bf16[512,256]{1,0:T(8,128)(2,1)S(1)} %copy-done, bf16[512,256]{1,0:T(8,128)(2,1)S(1)} %collective-permute-done.refs_1_, ...), custom_call_target="tpu_custom_call" | custom-call | tf_op jit(solution)/shard_map/solve/pallas_call | solution.py:136
  35.9 0.1 collective-permute-start.7
  36.0 1.5 %collective-permute-done.7 = bf16[256,512]{1,0:T(8,128)(2,1)S(1)} collective-permute-done((bf16[256,512]{1,0:T(8,128)(2,1)S(1)}, bf16[256,512]{1,0:T(8,128)(2,1)S(1)}, u32[]{:S(2)}, u32[]{:S(2)}) %collective-permute-start.7) | collective-permute-done | bytes 262176 | tf_op jit(solution)/shard_map/ppermute | solution.py:181
  37.5 0.1 add_convert_fusion
  37.6 12.3 %all_to_all.12 = bf16[8,32,512]{2,1,0:T(8,128)(2,1)S(1)} all-to-all(bf16[8,32,512]{2,1,0:T(8,128)(2,1)S(1)} %bitcast.13), channel_id=1, replica_groups=mesh['layer'=4,'proc'=8] {'proc'}, dimensions={0} | all-to-all | bytes 524288 | tf_op jit(solution)/shard_map/all_to_all | solution.py:238
  50.0 1.6 %collective-permute-start.8 = (f32[32,512]{1,0:T(8,128)S(1)}, f32[32,512]{1,0:T(8,128)S(1)}, u32[]{:S(2)}, u32[]{:S(2)}) collective-permute-start(f32[32,512]{1,0:T(8,128)S(1)} %convert_reduce_fusion), channel_id=1, source_target_pairs={{0,16},{8,24},{16,0},{24,8},{1,17},{9,25},{17,1},{25,9},{2,18},{10... | collective-permute-start | bytes 196616 | tf_op jit(solution)/shard_map/ppermute | solution.py:181
  51.5 2.8 %collective-permute-done.8 = f32[32,512]{1,0:T(8,128)S(1)} collective-permute-done((f32[32,512]{1,0:T(8,128)S(1)}, f32[32,512]{1,0:T(8,128)S(1)}, u32[]{:S(2)}, u32[]{:S(2)}) %collective-permute-start.8) | collective-permute-done | bytes 65568 | tf_op jit(solution)/shard_map/ppermute | solution.py:181
  54.3 0.0 copy-done.3
  54.3 0.1 collective-permute-start.9
  54.4 0.7 %dynamic-slice_bitcast_fusion = bf16[1536,32]{0,1:T(8,128)(2,1)} fusion(bf16[256,1536]{1,0:T(8,128)(2,1)S(1)} %get-tuple-element.14, s32[]{:T(128)S(6)} %select_n.13), kind=kLoop, calls=%fused_computation.2 | loop fusion | bytes 196612 | tf_op jit(solution)/shard_map/transpose | solution.py:246
  55.0 0.5 collective-permute-done.9.other_ref
  55.6 0.0 copy-done.1
  55.6 0.9 %ancestor.1 = f32[32,1024]{1,0:T(8,128)} custom-call(bf16[32,512]{1,0:T(8,128)(2,1)S(1)} %fusion.mine_ref, bf16[32,512]{1,0:T(8,128)(2,1)S(1)} %collective-permute-done.9.other_ref, bf16[1024,256]{1,0:T(8,128)(2,1)S(1)} %copy-done.1), custom_call_target="tpu_custom_call" | custom-call | tf_op jit(solution)/shard_map/ancestor/pallas_call | solution.py:170
  (2 shorter events, 0.1 us)
Async XLA Ops:
  0.6 33.0 %copy-start.2 = (s32[1,6]{1,0:T(1,128)S(1)}, s32[1,6]{1,0:T(1,128)}, u32[]{:S(2)}) copy-start(s32[1,6]{1,0:T(1,128)} %owner_ref.1) | copy-start | bytes 76
  2.7 30.9 %copy-start = (bf16[512,256]{1,0:T(8,128)(2,1)S(1)}, bf16[512,256]{1,0:T(8,128)(2,1)}, u32[]{:S(2)}) copy-start(bf16[512,256]{1,0:T(8,128)(2,1)} %operators.1.refs_0_) | copy-start | bytes 786436
  2.8 51.5 %copy-start.3 = (f32[1024,32]{0,1:T(8,128)S(1)}, f32[1024,32]{0,1:T(8,128)}, u32[]{:S(2)}) copy-start(f32[1024,32]{0,1:T(8,128)} %param.16) | copy-start | bytes 393220
  2.8 13.1 %collective-permute-start = (bf16[512,256]{1,0:T(8,128)(2,1)}, bf16[512,256]{1,0:T(8,128)(2,1)S(1)}, u32[]{:S(2)}, u32[]{:S(2)}) collective-permute-start(bf16[512,256]{1,0:T(8,128)(2,1)} %operators.1.refs_0_), channel_id=1, source_target_pairs={{0,1},{1,0},{2,3},{3,2},{4,5},{5,4},{6,7},{7,6},{8,9},{9,8},{10,11... | collective-permute-start | bytes 786440 | tf_op jit(solution)/shard_map/ppermute | solution.py:181
  5.8 11.3 %collective-permute-start.3 = (bf16[512,256]{1,0:T(8,128)(2,1)}, bf16[512,256]{1,0:T(8,128)(2,1)S(1)}, u32[]{:S(2)}, u32[]{:S(2)}) collective-permute-start(bf16[512,256]{1,0:T(8,128)(2,1)} %operators.1.refs_0_), channel_id=1, source_target_pairs={{0,6},{1,7},{2,4},{3,5},{4,2},{5,3},{6,0},{7,1},{8,14},{9,15},{10,... | collective-permute-start | bytes 786440 | tf_op jit(solution)/shard_map/ppermute | solution.py:181
  9.4 14.2 %collective-permute-start.1 = (bf16[512,256]{1,0:T(8,128)(2,1)}, bf16[512,256]{1,0:T(8,128)(2,1)S(1)}, u32[]{:S(2)}, u32[]{:S(2)}) collective-permute-start(bf16[512,256]{1,0:T(8,128)(2,1)} %operators.1.refs_0_), channel_id=1, source_target_pairs={{0,2},{1,3},{2,0},{3,1},{4,6},{5,7},{6,4},{7,5},{8,10},{9,11},{10,... | collective-permute-start | bytes 786440 | tf_op jit(solution)/shard_map/ppermute | solution.py:181
  10.1 45.5 %copy-start.1 = (bf16[1024,256]{1,0:T(8,128)(2,1)S(1)}, bf16[1024,256]{1,0:T(8,128)(2,1)}, u32[]{:S(2)}) copy-start(bf16[1024,256]{1,0:T(8,128)(2,1)} %inverse_ref.1) | copy-start | bytes 1572868
  15.9 15.9 %collective-permute-start.5 = (bf16[512,256]{1,0:T(8,128)(2,1)S(1)}, bf16[512,256]{1,0:T(8,128)(2,1)S(1)}, u32[]{:S(2)}, u32[]{:S(2)}) collective-permute-start(bf16[512,256]{1,0:T(8,128)(2,1)S(1)} %collective-permute-done.refs_1_), channel_id=1, source_target_pairs={{0,4},{1,5},{2,6},{3,7},{4,0},{5,1},{6,2},{7,3},{8,12},{9,13},{10,... | collective-permute-start | bytes 786440 | tf_op jit(solution)/shard_map/ppermute | solution.py:181
  17.1 15.5 %collective-permute-start.4 = (bf16[512,256]{1,0:T(8,128)(2,1)S(1)}, bf16[512,256]{1,0:T(8,128)(2,1)S(1)}, u32[]{:S(2)}, u32[]{:S(2)}) collective-permute-start(bf16[512,256]{1,0:T(8,128)(2,1)S(1)} %collective-permute-done.3.refs_6_), channel_id=1, source_target_pairs={{0,2},{1,3},{2,0},{3,1},{4,6},{5,7},{6,4},{7,5},{8,10},{9,11},{10,... | collective-permute-start | bytes 786440 | tf_op jit(solution)/shard_map/ppermute | solution.py:181
  23.3 9.3 %collective-permute-start.6 = (bf16[512,256]{1,0:T(8,128)(2,1)S(1)}, bf16[512,256]{1,0:T(8,128)(2,1)S(1)}, u32[]{:S(2)}, u32[]{:S(2)}) collective-permute-start(bf16[512,256]{1,0:T(8,128)(2,1)S(1)} %collective-permute-done.3.refs_6_), channel_id=1, source_target_pairs={{0,1},{1,0},{2,3},{3,2},{4,5},{5,4},{6,7},{7,6},{8,9},{9,8},{10,11... | collective-permute-start | bytes 786440 | tf_op jit(solution)/shard_map/ppermute | solution.py:181
  23.6 10.0 %collective-permute-start.2 = (bf16[512,256]{1,0:T(8,128)(2,1)S(1)}, bf16[512,256]{1,0:T(8,128)(2,1)S(1)}, u32[]{:S(2)}, u32[]{:S(2)}) collective-permute-start(bf16[512,256]{1,0:T(8,128)(2,1)S(1)} %collective-permute-done.1.refs_2_), channel_id=1, source_target_pairs={{0,1},{1,0},{2,3},{3,2},{4,5},{5,4},{6,7},{7,6},{8,9},{9,8},{10,11... | collective-permute-start | bytes 786440 | tf_op jit(solution)/shard_map/ppermute | solution.py:181
  35.9 1.6 %collective-permute-start.7 = (bf16[256,512]{1,0:T(8,128)(2,1)S(1)}, bf16[256,512]{1,0:T(8,128)(2,1)S(1)}, u32[]{:S(2)}, u32[]{:S(2)}) collective-permute-start(bf16[256,512]{1,0:T(8,128)(2,1)S(1)} %get-tuple-element.13), channel_id=1, source_target_pairs={{0,8},{8,0},{16,24},{24,16},{1,9},{9,1},{17,25},{25,17},{2,10},{10... | collective-permute-start | bytes 786440 | tf_op jit(solution)/shard_map/ppermute | solution.py:181
  50.0 4.3 %collective-permute-start.8 = (f32[32,512]{1,0:T(8,128)S(1)}, f32[32,512]{1,0:T(8,128)S(1)}, u32[]{:S(2)}, u32[]{:S(2)}) collective-permute-start(f32[32,512]{1,0:T(8,128)S(1)} %convert_reduce_fusion), channel_id=1, source_target_pairs={{0,16},{8,24},{16,0},{24,8},{1,17},{9,25},{17,1},{25,9},{2,18},{10... | collective-permute-start | bytes 196616 | tf_op jit(solution)/shard_map/ppermute | solution.py:181
  54.3 1.3 %collective-permute-start.9 = (bf16[32,512]{1,0:T(8,128)(2,1)S(1)}, bf16[32,512]{1,0:T(8,128)(2,1)S(1)}, u32[]{:S(2)}, u32[]{:S(2)}) collective-permute-start(bf16[32,512]{1,0:T(8,128)(2,1)S(1)} %fusion.mine_ref), channel_id=1, source_target_pairs={{0,8},{8,0},{16,24},{24,16},{1,9},{9,1},{17,25},{25,17},{2,10},{10... | collective-permute-start | bytes 98312 | tf_op jit(solution)/shard_map/ppermute | solution.py:181

commit v3 on v2

--- a/solution.py
+++ b/solution.py
@@ -11,7 +11,6 @@
 F32 = jnp.float32
 VMEM_LIMIT = 24 * 1024 * 1024
 SMALL_LIMIT = 8 * 1024 * 1024
-OPERATOR_LIMIT = 60 * 1024 * 1024
 GROUP_LIMIT = 50 * 1024 * 1024
 
 
@@ -39,14 +38,14 @@
 
 def operators(diag_inverse, chain_blocks, rhs_blocks):
     block = chain_blocks.shape[0]
-    inputs = (diag_inverse, chain_blocks, rhs_blocks)
+    inputs = [pltpu.with_memory_space_constraint(i, pltpu.HBM) for i in (diag_inverse, chain_blocks, rhs_blocks)]
     return pl.pallas_call(
         operator_kernel,
         out_shape=jax.ShapeDtypeStruct((block + rhs_blocks.shape[1], block), BF16),
         in_specs=[pl.BlockSpec(memory_space=pl.ANY)] * 3,
         out_specs=vmem_spec(),
         scratch_shapes=[pltpu.VMEM(i.shape, BF16) for i in inputs] + [pltpu.SemaphoreType.DMA((3,))],
-        compiler_params=pltpu.CompilerParams(vmem_limit_bytes=OPERATOR_LIMIT),
+        compiler_params=pltpu.CompilerParams(vmem_limit_bytes=SMALL_LIMIT),
         name="operators",
     )(*inputs)
 

time: 56.7 us -> 55.8 us (0.984)
  Pallas kernels: 11.1 us -> 10.4 us
    pallas_call x1, Pallas kernels: 2.1 us -> 1.4 us  [operators(): pl.pallas_call(operator_kernel, out_shape=jax.ShapeDtypeStruct((block + r...]
where the time goes in v3:
time: 55.8 us; the launch traced here: 55.6 us
  starting transfers between devices  17.3 us (31%)
  waiting for transfers between devices  13.4 us (24%)
  blocking collectives  12.3 us (22%)
  Pallas kernels  10.4 us (19%)
  other arithmetic  0.81 us (1%)
  between operations  0.71 us (1%)
  local copies, waits for them, and re-layouts  0.67 us (1%)
    ppermute x10, starting transfers between devices, exchange(): return lax.ppermute(value, axis, [(i, i ^ mask) for i in range(size)])  17.3 us
    ppermute x10, waiting for transfers between devices, exchange(): return lax.ppermute(value, axis, [(i, i ^ mask) for i in range(size)])  13.4 us
    all_to_all x1, blocking collectives, per_device(): parts = lax.all_to_all(total, 'proc', 0, 0, tiled=True)  12.3 us
    pallas_call x1, Pallas kernels, grouped(): pl.pallas_call(functools.partial(group_kernel, ticks, anc_count), out_sha...  5.75 us
    pallas_call x1, Pallas kernels, solve(): pl.pallas_call(functools.partial(solve_kernel, ticks), out_shape=(jax.Sha...  2.31 us
    pallas_call x1, Pallas kernels, operators(): pl.pallas_call(operator_kernel, out_shape=jax.ShapeDtypeStruct((block + r...  1.4 us
  transfers between devices with their start and end apart: 10, of which 7 were waited for; matrix products, arithmetic and copies ran while one was open for 2% of the time, Pallas kernels for 10%

profile of v3, /device:TPU:0, one launch (start us, length us, event | category | flops | bytes accessed | tf_op | source)
XLA Modules:
  0.0 55.6 jit_solution(13260726414666192212)
XLA Ops:
  0.6 0.0 copy-start.1
  0.6 1.4 %operators.1.refs_0_ = bf16[512,256]{1,0:T(8,128)(2,1)S(1)} custom-call(bf16[256,256]{1,0:T(8,128)(2,1)} %diag_ref.1, bf16[256,256]{1,0:T(8,128)(2,1)} %chain_ref.1, bf16[256,256]{1,0:T(8,128)(2,1)} %rhs_ref.1), custom_call_target="tpu_custom_call" | custom-call | tf_op jit(solution)/shard_map/operators/pallas_call | solution.py:42
  2.0 0.0 copy-start.2
  2.1 3.0 %collective-permute-start = (bf16[512,256]{1,0:T(8,128)(2,1)S(1)}, bf16[512,256]{1,0:T(8,128)(2,1)S(1)}, u32[]{:S(2)}, u32[]{:S(2)}) collective-permute-start(bf16[512,256]{1,0:T(8,128)(2,1)S(1)} %operators.1.refs_0_), channel_id=1, source_target_pairs={{0,1},{1,0},{2,3},{3,2},{4,5},{5,4},{6,7},{7,6},{8,9},{9,8},{10,11... | collective-permute-start | bytes 786440 | tf_op jit(solution)/shard_map/ppermute | solution.py:180
  5.1 3.6 %collective-permute-start.3 = (bf16[512,256]{1,0:T(8,128)(2,1)S(1)}, bf16[512,256]{1,0:T(8,128)(2,1)S(1)}, u32[]{:S(2)}, u32[]{:S(2)}) collective-permute-start(bf16[512,256]{1,0:T(8,128)(2,1)S(1)} %operators.1.refs_0_), channel_id=1, source_target_pairs={{0,6},{1,7},{2,4},{3,5},{4,2},{5,3},{6,0},{7,1},{8,14},{9,15},{10,... | collective-permute-start | bytes 786440 | tf_op jit(solution)/shard_map/ppermute | solution.py:180
  8.7 0.0 collective-permute-start.1
  8.7 0.7 %add_bitcast_fusion.pair_ref = s32[80]{0:T(128)S(1)} fusion(s32[1,80]{1,0:T(1,128)} %param.14, s32[1,80]{1,0:T(1,128)} %param.15), kind=kLoop, calls=%fused_computation.5 | loop fusion | flops 160 | bytes 960 | tf_op jit(solution)/shard_map/add | solution.py:232
  9.4 0.0 copy-start
  9.4 5.8 %grouped.1.group_ref = bf16[1536,1024]{1,0:T(8,128)(2,1)S(1)} custom-call(s32[80]{0:T(128)S(1)} %add_bitcast_fusion.pair_ref, bf16[20480,256]{1,0:T(8,128)(2,1)} %factor_ref.1), custom_call_target="tpu_custom_call" | custom-call | flops 5242880 | bytes 10485760 | tf_op jit(solution)/shard_map/grouped/pallas_call | solution.py:83
  15.1 0.0 collective-permute-done.refs_1_
  15.1 0.8 %collective-permute-start.5 = (bf16[512,256]{1,0:T(8,128)(2,1)S(1)}, bf16[512,256]{1,0:T(8,128)(2,1)S(1)}, u32[]{:S(2)}, u32[]{:S(2)}) collective-permute-start(bf16[512,256]{1,0:T(8,128)(2,1)S(1)} %collective-permute-done.refs_1_), channel_id=1, source_target_pairs={{0,4},{1,5},{2,6},{3,7},{4,0},{5,1},{6,2},{7,3},{8,12},{9,13},{10,... | collective-permute-start | bytes 786440 | tf_op jit(solution)/shard_map/ppermute | solution.py:180
  16.0 0.2 collective-permute-done.3.refs_6_
  16.2 6.1 %collective-permute-start.4 = (bf16[512,256]{1,0:T(8,128)(2,1)S(1)}, bf16[512,256]{1,0:T(8,128)(2,1)S(1)}, u32[]{:S(2)}, u32[]{:S(2)}) collective-permute-start(bf16[512,256]{1,0:T(8,128)(2,1)S(1)} %collective-permute-done.3.refs_6_), channel_id=1, source_target_pairs={{0,2},{1,3},{2,0},{3,1},{4,6},{5,7},{6,4},{7,5},{8,10},{9,11},{10,... | collective-permute-start | bytes 786440 | tf_op jit(solution)/shard_map/ppermute | solution.py:180
  22.3 0.4 collective-permute-start.6
  22.7 0.0 collective-permute-done.1.refs_2_
  22.7 1.6 %collective-permute-start.2 = (bf16[512,256]{1,0:T(8,128)(2,1)S(1)}, bf16[512,256]{1,0:T(8,128)(2,1)S(1)}, u32[]{:S(2)}, u32[]{:S(2)}) collective-permute-start(bf16[512,256]{1,0:T(8,128)(2,1)S(1)} %collective-permute-done.1.refs_2_), channel_id=1, source_target_pairs={{0,1},{1,0},{2,3},{3,2},{4,5},{5,4},{6,7},{7,6},{8,9},{9,8},{10,11... | collective-permute-start | bytes 786440 | tf_op jit(solution)/shard_map/ppermute | solution.py:180
  24.3 6.5 %collective-permute-done.5.refs_5_ = bf16[512,256]{1,0:T(8,128)(2,1)S(1)} collective-permute-done((bf16[512,256]{1,0:T(8,128)(2,1)S(1)}, bf16[512,256]{1,0:T(8,128)(2,1)S(1)}, u32[]{:S(2)}, u32[]{:S(2)}) %collective-permute-start.5) | collective-permute-done | bytes 262176 | tf_op jit(solution)/shard_map/ppermute | solution.py:180
  30.8 0.8 %collective-permute-done.4.refs_4_ = bf16[512,256]{1,0:T(8,128)(2,1)S(1)} collective-permute-done((bf16[512,256]{1,0:T(8,128)(2,1)S(1)}, bf16[512,256]{1,0:T(8,128)(2,1)S(1)}, u32[]{:S(2)}, u32[]{:S(2)}) %collective-permute-start.4) | collective-permute-done | bytes 262176 | tf_op jit(solution)/shard_map/ppermute | solution.py:180
  31.7 0.0 collective-permute-done.6.refs_7_
  31.7 1.0 %collective-permute-done.2.refs_3_ = bf16[512,256]{1,0:T(8,128)(2,1)S(1)} collective-permute-done((bf16[512,256]{1,0:T(8,128)(2,1)S(1)}, bf16[512,256]{1,0:T(8,128)(2,1)S(1)}, u32[]{:S(2)}, u32[]{:S(2)}) %collective-permute-start.2) | collective-permute-done | bytes 262176 | tf_op jit(solution)/shard_map/ppermute | solution.py:180
  32.7 0.0 copy-done.1
  32.7 2.3 %solve.1 = (bf16[256,1536]{1,0:T(8,128)(2,1)S(1)}, bf16[256,512]{1,0:T(8,128)(2,1)S(1)}, f32[256,512]{1,0:T(8,128)S(1)}) custom-call(s32[1,6]{1,0:T(1,128)S(1)} %copy-done.1, bf16[1536,1024]{1,0:T(8,128)(2,1)S(1)} %grouped.1.group_ref, bf16[512,256]{1,0:T(8,128)(2,1)S(1)} %operators.1.refs_0_, bf16[512,256]{1,0:T(8,128)(2,1)S(1)} %collective-permute-done.refs_1_, ...), custom_call_target="tpu_custom_call" | custom-call | tf_op jit(solution)/shard_map/solve/pallas_call | solution.py:135
  35.0 0.1 collective-permute-start.7
  35.1 1.5 %collective-permute-done.7 = bf16[256,512]{1,0:T(8,128)(2,1)S(1)} collective-permute-done((bf16[256,512]{1,0:T(8,128)(2,1)S(1)}, bf16[256,512]{1,0:T(8,128)(2,1)S(1)}, u32[]{:S(2)}, u32[]{:S(2)}) %collective-permute-start.7) | collective-permute-done | bytes 262176 | tf_op jit(solution)/shard_map/ppermute | solution.py:180
  36.6 0.1 add_convert_fusion
  36.7 12.3 %all_to_all.12 = bf16[8,32,512]{2,1,0:T(8,128)(2,1)S(1)} all-to-all(bf16[8,32,512]{2,1,0:T(8,128)(2,1)S(1)} %bitcast.13), channel_id=1, replica_groups=mesh['layer'=4,'proc'=8] {'proc'}, dimensions={0} | all-to-all | bytes 524288 | tf_op jit(solution)/shard_map/all_to_all | solution.py:237
  49.0 1.6 %collective-permute-start.8 = (f32[32,512]{1,0:T(8,128)S(1)}, f32[32,512]{1,0:T(8,128)S(1)}, u32[]{:S(2)}, u32[]{:S(2)}) collective-permute-start(f32[32,512]{1,0:T(8,128)S(1)} %convert_reduce_fusion), channel_id=1, source_target_pairs={{0,16},{8,24},{16,0},{24,8},{1,17},{9,25},{17,1},{25,9},{2,18},{10... | collective-permute-start | bytes 196616 | tf_op jit(solution)/shard_map/ppermute | solution.py:180
  50.6 2.8 %collective-permute-done.8 = f32[32,512]{1,0:T(8,128)S(1)} collective-permute-done((f32[32,512]{1,0:T(8,128)S(1)}, f32[32,512]{1,0:T(8,128)S(1)}, u32[]{:S(2)}, u32[]{:S(2)}) %collective-permute-start.8) | collective-permute-done | bytes 65568 | tf_op jit(solution)/shard_map/ppermute | solution.py:180
  53.4 0.0 copy-done.2
  53.4 0.1 collective-permute-start.9
  53.5 0.7 %dynamic-slice_bitcast_fusion = bf16[1536,32]{0,1:T(8,128)(2,1)} fusion(bf16[256,1536]{1,0:T(8,128)(2,1)S(1)} %get-tuple-element.14, s32[]{:T(128)S(6)} %select_n.13), kind=kLoop, calls=%fused_computation.2 | loop fusion | bytes 196612 | tf_op jit(solution)/shard_map/transpose | solution.py:245
  54.1 0.5 collective-permute-done.9.other_ref
  54.7 0.0 copy-done
  54.7 0.9 %ancestor.1 = f32[32,1024]{1,0:T(8,128)} custom-call(bf16[32,512]{1,0:T(8,128)(2,1)S(1)} %fusion.mine_ref, bf16[32,512]{1,0:T(8,128)(2,1)S(1)} %collective-permute-done.9.other_ref, bf16[1024,256]{1,0:T(8,128)(2,1)S(1)} %copy-done), custom_call_target="tpu_custom_call" | custom-call | tf_op jit(solution)/shard_map/ancestor/pallas_call | solution.py:169
  (2 shorter events, 0.1 us)
Async XLA Ops:
  0.6 32.1 %copy-start.1 = (s32[1,6]{1,0:T(1,128)S(1)}, s32[1,6]{1,0:T(1,128)}, u32[]{:S(2)}) copy-start(s32[1,6]{1,0:T(1,128)} %owner_ref.1) | copy-start | bytes 76
  2.0 51.3 %copy-start.2 = (f32[1024,32]{0,1:T(8,128)S(1)}, f32[1024,32]{0,1:T(8,128)}, u32[]{:S(2)}) copy-start(f32[1024,32]{0,1:T(8,128)} %param.16) | copy-start | bytes 393220
  2.1 13.1 %collective-permute-start = (bf16[512,256]{1,0:T(8,128)(2,1)S(1)}, bf16[512,256]{1,0:T(8,128)(2,1)S(1)}, u32[]{:S(2)}, u32[]{:S(2)}) collective-permute-start(bf16[512,256]{1,0:T(8,128)(2,1)S(1)} %operators.1.refs_0_), channel_id=1, source_target_pairs={{0,1},{1,0},{2,3},{3,2},{4,5},{5,4},{6,7},{7,6},{8,9},{9,8},{10,11... | collective-permute-start | bytes 786440 | tf_op jit(solution)/shard_map/ppermute | solution.py:180
  5.1 11.1 %collective-permute-start.3 = (bf16[512,256]{1,0:T(8,128)(2,1)S(1)}, bf16[512,256]{1,0:T(8,128)(2,1)S(1)}, u32[]{:S(2)}, u32[]{:S(2)}) collective-permute-start(bf16[512,256]{1,0:T(8,128)(2,1)S(1)} %operators.1.refs_0_), channel_id=1, source_target_pairs={{0,6},{1,7},{2,4},{3,5},{4,2},{5,3},{6,0},{7,1},{8,14},{9,15},{10,... | collective-permute-start | bytes 786440 | tf_op jit(solution)/shard_map/ppermute | solution.py:180
  8.7 14.0 %collective-permute-start.1 = (bf16[512,256]{1,0:T(8,128)(2,1)S(1)}, bf16[512,256]{1,0:T(8,128)(2,1)S(1)}, u32[]{:S(2)}, u32[]{:S(2)}) collective-permute-start(bf16[512,256]{1,0:T(8,128)(2,1)S(1)} %operators.1.refs_0_), channel_id=1, source_target_pairs={{0,2},{1,3},{2,0},{3,1},{4,6},{5,7},{6,4},{7,5},{8,10},{9,11},{10,... | collective-permute-start | bytes 786440 | tf_op jit(solution)/shard_map/ppermute | solution.py:180
  9.4 45.3 %copy-start = (bf16[1024,256]{1,0:T(8,128)(2,1)S(1)}, bf16[1024,256]{1,0:T(8,128)(2,1)}, u32[]{:S(2)}) copy-start(bf16[1024,256]{1,0:T(8,128)(2,1)} %inverse_ref.1) | copy-start | bytes 1572868
  15.1 15.7 %collective-permute-start.5 = (bf16[512,256]{1,0:T(8,128)(2,1)S(1)}, bf16[512,256]{1,0:T(8,128)(2,1)S(1)}, u32[]{:S(2)}, u32[]{:S(2)}) collective-permute-start(bf16[512,256]{1,0:T(8,128)(2,1)S(1)} %collective-permute-done.refs_1_), channel_id=1, source_target_pairs={{0,4},{1,5},{2,6},{3,7},{4,0},{5,1},{6,2},{7,3},{8,12},{9,13},{10,... | collective-permute-start | bytes 786440 | tf_op jit(solution)/shard_map/ppermute | solution.py:180
  16.2 15.5 %collective-permute-start.4 = (bf16[512,256]{1,0:T(8,128)(2,1)S(1)}, bf16[512,256]{1,0:T(8,128)(2,1)S(1)}, u32[]{:S(2)}, u32[]{:S(2)}) collective-permute-start(bf16[512,256]{1,0:T(8,128)(2,1)S(1)} %collective-permute-done.3.refs_6_), channel_id=1, source_target_pairs={{0,2},{1,3},{2,0},{3,1},{4,6},{5,7},{6,4},{7,5},{8,10},{9,11},{10,... | collective-permute-start | bytes 786440 | tf_op jit(solution)/shard_map/ppermute | solution.py:180
  22.3 9.4 %collective-permute-start.6 = (bf16[512,256]{1,0:T(8,128)(2,1)S(1)}, bf16[512,256]{1,0:T(8,128)(2,1)S(1)}, u32[]{:S(2)}, u32[]{:S(2)}) collective-permute-start(bf16[512,256]{1,0:T(8,128)(2,1)S(1)} %collective-permute-done.3.refs_6_), channel_id=1, source_target_pairs={{0,1},{1,0},{2,3},{3,2},{4,5},{5,4},{6,7},{7,6},{8,9},{9,8},{10,11... | collective-permute-start | bytes 786440 | tf_op jit(solution)/shard_map/ppermute | solution.py:180
  22.7 10.0 %collective-permute-start.2 = (bf16[512,256]{1,0:T(8,128)(2,1)S(1)}, bf16[512,256]{1,0:T(8,128)(2,1)S(1)}, u32[]{:S(2)}, u32[]{:S(2)}) collective-permute-start(bf16[512,256]{1,0:T(8,128)(2,1)S(1)} %collective-permute-done.1.refs_2_), channel_id=1, source_target_pairs={{0,1},{1,0},{2,3},{3,2},{4,5},{5,4},{6,7},{7,6},{8,9},{9,8},{10,11... | collective-permute-start | bytes 786440 | tf_op jit(solution)/shard_map/ppermute | solution.py:180
  35.0 1.6 %collective-permute-start.7 = (bf16[256,512]{1,0:T(8,128)(2,1)S(1)}, bf16[256,512]{1,0:T(8,128)(2,1)S(1)}, u32[]{:S(2)}, u32[]{:S(2)}) collective-permute-start(bf16[256,512]{1,0:T(8,128)(2,1)S(1)} %get-tuple-element.13), channel_id=1, source_target_pairs={{0,8},{8,0},{16,24},{24,16},{1,9},{9,1},{17,25},{25,17},{2,10},{10... | collective-permute-start | bytes 786440 | tf_op jit(solution)/shard_map/ppermute | solution.py:180
  49.0 4.3 %collective-permute-start.8 = (f32[32,512]{1,0:T(8,128)S(1)}, f32[32,512]{1,0:T(8,128)S(1)}, u32[]{:S(2)}, u32[]{:S(2)}) collective-permute-start(f32[32,512]{1,0:T(8,128)S(1)} %convert_reduce_fusion), channel_id=1, source_target_pairs={{0,16},{8,24},{16,0},{24,8},{1,17},{9,25},{17,1},{25,9},{2,18},{10... | collective-permute-start | bytes 196616 | tf_op jit(solution)/shard_map/ppermute | solution.py:180
  53.4 1.3 %collective-permute-start.9 = (bf16[32,512]{1,0:T(8,128)(2,1)S(1)}, bf16[32,512]{1,0:T(8,128)(2,1)S(1)}, u32[]{:S(2)}, u32[]{:S(2)}) collective-permute-start(bf16[32,512]{1,0:T(8,128)(2,1)S(1)} %fusion.mine_ref), channel_id=1, source_target_pairs={{0,8},{8,0},{16,24},{24,16},{1,9},{9,1},{17,25},{25,17},{2,10},{10... | collective-permute-start | bytes 98312 | tf_op jit(solution)/shard_map/ppermute | solution.py:180

commit v4 on v3

--- a/solution.py
+++ b/solution.py
@@ -238,7 +238,8 @@
     solved_t, parts = lax.optimization_barrier((solved_t, parts))
     total = jnp.sum(parts.reshape(procs, columns, half).astype(F32), axis=0)
     for k in range(1, layers.bit_length() - 1):
-        total = total + exchange(total, "layer", layers, 1 << k)
+        total = total.astype(BF16)
+        total = total.astype(F32) + exchange(total, "layer", layers, 1 << k).astype(F32)
     anc_t = lax.dynamic_slice_in_dim(anc_rhs, layer % 2 * half, half, 0).T
     mine = (anc_t - total).astype(BF16)
     ancestor = solve_ancestor(mine, exchange(mine, "layer", layers, 1), anc_inverse).T

time: 55.8 us -> 55.4 us (level)
  no operation moved by 1% of the time
where the time goes in v4:
time: 55.4 us; the launch traced here: 55.3 us
  starting transfers between devices  17.3 us (31%)
  waiting for transfers between devices  13.1 us (24%)
  blocking collectives  12.3 us (22%)
  Pallas kernels  10.4 us (19%)
  other arithmetic  0.81 us (1%)
  between operations  0.72 us (1%)
  local copies, waits for them, and re-layouts  0.67 us (1%)
    ppermute x10, starting transfers between devices, exchange(): return lax.ppermute(value, axis, [(i, i ^ mask) for i in range(size)])  17.3 us
    ppermute x10, waiting for transfers between devices, exchange(): return lax.ppermute(value, axis, [(i, i ^ mask) for i in range(size)])  13.1 us
    all_to_all x1, blocking collectives, per_device(): parts = lax.all_to_all(total, 'proc', 0, 0, tiled=True)  12.3 us
    pallas_call x1, Pallas kernels, grouped(): pl.pallas_call(functools.partial(group_kernel, ticks, anc_count), out_sha...  5.75 us
    pallas_call x1, Pallas kernels, solve(): pl.pallas_call(functools.partial(solve_kernel, ticks), out_shape=(jax.Sha...  2.31 us
    pallas_call x1, Pallas kernels, operators(): pl.pallas_call(operator_kernel, out_shape=jax.ShapeDtypeStruct((block + r...  1.4 us
  transfers between devices with their start and end apart: 10, of which 7 were waited for; matrix products, arithmetic and copies ran while one was open for 2% of the time, Pallas kernels for 10%

profile of v4, /device:TPU:0, one launch (start us, length us, event | category | flops | bytes accessed | tf_op | source)
XLA Modules:
  0.0 55.3 jit_solution(9276803455437300237)
XLA Ops:
  0.6 0.0 copy-start.1
  0.6 1.4 %operators.1.refs_0_ = bf16[512,256]{1,0:T(8,128)(2,1)S(1)} custom-call(bf16[256,256]{1,0:T(8,128)(2,1)} %diag_ref.1, bf16[256,256]{1,0:T(8,128)(2,1)} %chain_ref.1, bf16[256,256]{1,0:T(8,128)(2,1)} %rhs_ref.1), custom_call_target="tpu_custom_call" | custom-call | tf_op jit(solution)/shard_map/operators/pallas_call | solution.py:42
  2.0 0.0 copy-start.2
  2.1 3.0 %collective-permute-start = (bf16[512,256]{1,0:T(8,128)(2,1)S(1)}, bf16[512,256]{1,0:T(8,128)(2,1)S(1)}, u32[]{:S(2)}, u32[]{:S(2)}) collective-permute-start(bf16[512,256]{1,0:T(8,128)(2,1)S(1)} %operators.1.refs_0_), channel_id=1, source_target_pairs={{0,1},{1,0},{2,3},{3,2},{4,5},{5,4},{6,7},{7,6},{8,9},{9,8},{10,11... | collective-permute-start | bytes 786440 | tf_op jit(solution)/shard_map/ppermute | solution.py:180
  5.1 3.6 %collective-permute-start.3 = (bf16[512,256]{1,0:T(8,128)(2,1)S(1)}, bf16[512,256]{1,0:T(8,128)(2,1)S(1)}, u32[]{:S(2)}, u32[]{:S(2)}) collective-permute-start(bf16[512,256]{1,0:T(8,128)(2,1)S(1)} %operators.1.refs_0_), channel_id=1, source_target_pairs={{0,6},{1,7},{2,4},{3,5},{4,2},{5,3},{6,0},{7,1},{8,14},{9,15},{10,... | collective-permute-start | bytes 786440 | tf_op jit(solution)/shard_map/ppermute | solution.py:180
  8.7 0.0 collective-permute-start.1
  8.7 0.7 %add_bitcast_fusion.pair_ref = s32[80]{0:T(128)S(1)} fusion(s32[1,80]{1,0:T(1,128)} %param.14, s32[1,80]{1,0:T(1,128)} %param.15), kind=kLoop, calls=%fused_computation.4 | loop fusion | flops 160 | bytes 960 | tf_op jit(solution)/shard_map/add | solution.py:232
  9.4 0.0 copy-start
  9.4 5.8 %grouped.1.group_ref = bf16[1536,1024]{1,0:T(8,128)(2,1)S(1)} custom-call(s32[80]{0:T(128)S(1)} %add_bitcast_fusion.pair_ref, bf16[20480,256]{1,0:T(8,128)(2,1)} %factor_ref.1), custom_call_target="tpu_custom_call" | custom-call | flops 5242880 | bytes 10485760 | tf_op jit(solution)/shard_map/grouped/pallas_call | solution.py:83
  15.1 0.0 collective-permute-done.refs_1_
  15.1 0.8 %collective-permute-start.5 = (bf16[512,256]{1,0:T(8,128)(2,1)S(1)}, bf16[512,256]{1,0:T(8,128)(2,1)S(1)}, u32[]{:S(2)}, u32[]{:S(2)}) collective-permute-start(bf16[512,256]{1,0:T(8,128)(2,1)S(1)} %collective-permute-done.refs_1_), channel_id=1, source_target_pairs={{0,4},{1,5},{2,6},{3,7},{4,0},{5,1},{6,2},{7,3},{8,12},{9,13},{10,... | collective-permute-start | bytes 786440 | tf_op jit(solution)/shard_map/ppermute | solution.py:180
  16.0 0.2 collective-permute-done.3.refs_6_
  16.2 6.1 %collective-permute-start.4 = (bf16[512,256]{1,0:T(8,128)(2,1)S(1)}, bf16[512,256]{1,0:T(8,128)(2,1)S(1)}, u32[]{:S(2)}, u32[]{:S(2)}) collective-permute-start(bf16[512,256]{1,0:T(8,128)(2,1)S(1)} %collective-permute-done.3.refs_6_), channel_id=1, source_target_pairs={{0,2},{1,3},{2,0},{3,1},{4,6},{5,7},{6,4},{7,5},{8,10},{9,11},{10,... | collective-permute-start | bytes 786440 | tf_op jit(solution)/shard_map/ppermute | solution.py:180
  22.3 0.4 collective-permute-start.6
  22.7 0.0 collective-permute-done.1.refs_2_
  22.7 1.6 %collective-permute-start.2 = (bf16[512,256]{1,0:T(8,128)(2,1)S(1)}, bf16[512,256]{1,0:T(8,128)(2,1)S(1)}, u32[]{:S(2)}, u32[]{:S(2)}) collective-permute-start(bf16[512,256]{1,0:T(8,128)(2,1)S(1)} %collective-permute-done.1.refs_2_), channel_id=1, source_target_pairs={{0,1},{1,0},{2,3},{3,2},{4,5},{5,4},{6,7},{7,6},{8,9},{9,8},{10,11... | collective-permute-start | bytes 786440 | tf_op jit(solution)/shard_map/ppermute | solution.py:180
  24.3 6.5 %collective-permute-done.5.refs_5_ = bf16[512,256]{1,0:T(8,128)(2,1)S(1)} collective-permute-done((bf16[512,256]{1,0:T(8,128)(2,1)S(1)}, bf16[512,256]{1,0:T(8,128)(2,1)S(1)}, u32[]{:S(2)}, u32[]{:S(2)}) %collective-permute-start.5) | collective-permute-done | bytes 262176 | tf_op jit(solution)/shard_map/ppermute | solution.py:180
  30.8 0.8 %collective-permute-done.4.refs_4_ = bf16[512,256]{1,0:T(8,128)(2,1)S(1)} collective-permute-done((bf16[512,256]{1,0:T(8,128)(2,1)S(1)}, bf16[512,256]{1,0:T(8,128)(2,1)S(1)}, u32[]{:S(2)}, u32[]{:S(2)}) %collective-permute-start.4) | collective-permute-done | bytes 262176 | tf_op jit(solution)/shard_map/ppermute | solution.py:180
  31.7 0.0 collective-permute-done.6.refs_7_
  31.7 1.0 %collective-permute-done.2.refs_3_ = bf16[512,256]{1,0:T(8,128)(2,1)S(1)} collective-permute-done((bf16[512,256]{1,0:T(8,128)(2,1)S(1)}, bf16[512,256]{1,0:T(8,128)(2,1)S(1)}, u32[]{:S(2)}, u32[]{:S(2)}) %collective-permute-start.2) | collective-permute-done | bytes 262176 | tf_op jit(solution)/shard_map/ppermute | solution.py:180
  32.7 0.0 copy-done.1
  32.7 2.3 %solve.1 = (bf16[256,1536]{1,0:T(8,128)(2,1)S(1)}, bf16[256,512]{1,0:T(8,128)(2,1)S(1)}, f32[256,512]{1,0:T(8,128)S(1)}) custom-call(s32[1,6]{1,0:T(1,128)S(1)} %copy-done.1, bf16[1536,1024]{1,0:T(8,128)(2,1)S(1)} %grouped.1.group_ref, bf16[512,256]{1,0:T(8,128)(2,1)S(1)} %operators.1.refs_0_, bf16[512,256]{1,0:T(8,128)(2,1)S(1)} %collective-permute-done.refs_1_, ...), custom_call_target="tpu_custom_call" | custom-call | tf_op jit(solution)/shard_map/solve/pallas_call | solution.py:135
  35.0 0.1 collective-permute-start.7
  35.1 1.5 %collective-permute-done.7 = bf16[256,512]{1,0:T(8,128)(2,1)S(1)} collective-permute-done((bf16[256,512]{1,0:T(8,128)(2,1)S(1)}, bf16[256,512]{1,0:T(8,128)(2,1)S(1)}, u32[]{:S(2)}, u32[]{:S(2)}) %collective-permute-start.7) | collective-permute-done | bytes 262176 | tf_op jit(solution)/shard_map/ppermute | solution.py:180
  36.6 0.1 add_convert_fusion
  36.7 12.3 %all_to_all.12 = bf16[8,32,512]{2,1,0:T(8,128)(2,1)S(1)} all-to-all(bf16[8,32,512]{2,1,0:T(8,128)(2,1)S(1)} %bitcast.12), channel_id=1, replica_groups=mesh['layer'=4,'proc'=8] {'proc'}, dimensions={0} | all-to-all | bytes 524288 | tf_op jit(solution)/shard_map/all_to_all | solution.py:237
  49.1 1.6 %collective-permute-start.8 = (bf16[32,512]{1,0:T(8,128)(2,1)S(1)}, bf16[32,512]{1,0:T(8,128)(2,1)S(1)}, u32[]{:S(2)}, u32[]{:S(2)}) collective-permute-start(bf16[32,512]{1,0:T(8,128)(2,1)S(1)} %reduce_sum.12), channel_id=1, source_target_pairs={{0,16},{8,24},{16,0},{24,8},{1,17},{9,25},{17,1},{25,9},{2,18},{10... | collective-permute-start | bytes 98312 | tf_op jit(solution)/shard_map/ppermute | solution.py:180
  50.6 2.4 %collective-permute-done.8 = bf16[32,512]{1,0:T(8,128)(2,1)S(1)} collective-permute-done((bf16[32,512]{1,0:T(8,128)(2,1)S(1)}, bf16[32,512]{1,0:T(8,128)(2,1)S(1)}, u32[]{:S(2)}, u32[]{:S(2)}) %collective-permute-start.8) | collective-permute-done | bytes 32800 | tf_op jit(solution)/shard_map/ppermute | solution.py:180
  53.0 0.0 copy-done.2
  53.1 0.1 collective-permute-start.9
  53.1 0.7 %dynamic-slice_bitcast_fusion = bf16[1536,32]{0,1:T(8,128)(2,1)} fusion(bf16[256,1536]{1,0:T(8,128)(2,1)S(1)} %get-tuple-element.14, s32[]{:T(128)S(6)} %select_n.13), kind=kLoop, calls=%fused_computation.1 | loop fusion | bytes 196612 | tf_op jit(solution)/shard_map/transpose | solution.py:246
  53.8 0.5 collective-permute-done.9.other_ref
  54.3 0.0 copy-done
  54.3 0.9 %ancestor.1 = f32[32,1024]{1,0:T(8,128)} custom-call(bf16[32,512]{1,0:T(8,128)(2,1)S(1)} %fusion.mine_ref, bf16[32,512]{1,0:T(8,128)(2,1)S(1)} %collective-permute-done.9.other_ref, bf16[1024,256]{1,0:T(8,128)(2,1)S(1)} %copy-done), custom_call_target="tpu_custom_call" | custom-call | tf_op jit(solution)/shard_map/ancestor/pallas_call | solution.py:169
  (2 shorter events, 0.1 us)
Async XLA Ops:
  0.6 32.1 %copy-start.1 = (s32[1,6]{1,0:T(1,128)S(1)}, s32[1,6]{1,0:T(1,128)}, u32[]{:S(2)}) copy-start(s32[1,6]{1,0:T(1,128)} %owner_ref.1) | copy-start | bytes 76
  2.0 51.0 %copy-start.2 = (f32[1024,32]{0,1:T(8,128)S(1)}, f32[1024,32]{0,1:T(8,128)}, u32[]{:S(2)}) copy-start(f32[1024,32]{0,1:T(8,128)} %param.16) | copy-start | bytes 393220
  2.1 13.1 %collective-permute-start = (bf16[512,256]{1,0:T(8,128)(2,1)S(1)}, bf16[512,256]{1,0:T(8,128)(2,1)S(1)}, u32[]{:S(2)}, u32[]{:S(2)}) collective-permute-start(bf16[512,256]{1,0:T(8,128)(2,1)S(1)} %operators.1.refs_0_), channel_id=1, source_target_pairs={{0,1},{1,0},{2,3},{3,2},{4,5},{5,4},{6,7},{7,6},{8,9},{9,8},{10,11... | collective-permute-start | bytes 786440 | tf_op jit(solution)/shard_map/ppermute | solution.py:180
  5.1 11.1 %collective-permute-start.3 = (bf16[512,256]{1,0:T(8,128)(2,1)S(1)}, bf16[512,256]{1,0:T(8,128)(2,1)S(1)}, u32[]{:S(2)}, u32[]{:S(2)}) collective-permute-start(bf16[512,256]{1,0:T(8,128)(2,1)S(1)} %operators.1.refs_0_), channel_id=1, source_target_pairs={{0,6},{1,7},{2,4},{3,5},{4,2},{5,3},{6,0},{7,1},{8,14},{9,15},{10,... | collective-permute-start | bytes 786440 | tf_op jit(solution)/shard_map/ppermute | solution.py:180
  8.7 14.0 %collective-permute-start.1 = (bf16[512,256]{1,0:T(8,128)(2,1)S(1)}, bf16[512,256]{1,0:T(8,128)(2,1)S(1)}, u32[]{:S(2)}, u32[]{:S(2)}) collective-permute-start(bf16[512,256]{1,0:T(8,128)(2,1)S(1)} %operators.1.refs_0_), channel_id=1, source_target_pairs={{0,2},{1,3},{2,0},{3,1},{4,6},{5,7},{6,4},{7,5},{8,10},{9,11},{10,... | collective-permute-start | bytes 786440 | tf_op jit(solution)/shard_map/ppermute | solution.py:180
  9.4 45.0 %copy-start = (bf16[1024,256]{1,0:T(8,128)(2,1)S(1)}, bf16[1024,256]{1,0:T(8,128)(2,1)}, u32[]{:S(2)}) copy-start(bf16[1024,256]{1,0:T(8,128)(2,1)} %inverse_ref.1) | copy-start | bytes 1572868
  15.1 15.7 %collective-permute-start.5 = (bf16[512,256]{1,0:T(8,128)(2,1)S(1)}, bf16[512,256]{1,0:T(8,128)(2,1)S(1)}, u32[]{:S(2)}, u32[]{:S(2)}) collective-permute-start(bf16[512,256]{1,0:T(8,128)(2,1)S(1)} %collective-permute-done.refs_1_), channel_id=1, source_target_pairs={{0,4},{1,5},{2,6},{3,7},{4,0},{5,1},{6,2},{7,3},{8,12},{9,13},{10,... | collective-permute-start | bytes 786440 | tf_op jit(solution)/shard_map/ppermute | solution.py:180
  16.2 15.5 %collective-permute-start.4 = (bf16[512,256]{1,0:T(8,128)(2,1)S(1)}, bf16[512,256]{1,0:T(8,128)(2,1)S(1)}, u32[]{:S(2)}, u32[]{:S(2)}) collective-permute-start(bf16[512,256]{1,0:T(8,128)(2,1)S(1)} %collective-permute-done.3.refs_6_), channel_id=1, source_target_pairs={{0,2},{1,3},{2,0},{3,1},{4,6},{5,7},{6,4},{7,5},{8,10},{9,11},{10,... | collective-permute-start | bytes 786440 | tf_op jit(solution)/shard_map/ppermute | solution.py:180
  22.3 9.4 %collective-permute-start.6 = (bf16[512,256]{1,0:T(8,128)(2,1)S(1)}, bf16[512,256]{1,0:T(8,128)(2,1)S(1)}, u32[]{:S(2)}, u32[]{:S(2)}) collective-permute-start(bf16[512,256]{1,0:T(8,128)(2,1)S(1)} %collective-permute-done.3.refs_6_), channel_id=1, source_target_pairs={{0,1},{1,0},{2,3},{3,2},{4,5},{5,4},{6,7},{7,6},{8,9},{9,8},{10,11... | collective-permute-start | bytes 786440 | tf_op jit(solution)/shard_map/ppermute | solution.py:180
  22.7 10.0 %collective-permute-start.2 = (bf16[512,256]{1,0:T(8,128)(2,1)S(1)}, bf16[512,256]{1,0:T(8,128)(2,1)S(1)}, u32[]{:S(2)}, u32[]{:S(2)}) collective-permute-start(bf16[512,256]{1,0:T(8,128)(2,1)S(1)} %collective-permute-done.1.refs_2_), channel_id=1, source_target_pairs={{0,1},{1,0},{2,3},{3,2},{4,5},{5,4},{6,7},{7,6},{8,9},{9,8},{10,11... | collective-permute-start | bytes 786440 | tf_op jit(solution)/shard_map/ppermute | solution.py:180
  35.0 1.6 %collective-permute-start.7 = (bf16[256,512]{1,0:T(8,128)(2,1)S(1)}, bf16[256,512]{1,0:T(8,128)(2,1)S(1)}, u32[]{:S(2)}, u32[]{:S(2)}) collective-permute-start(bf16[256,512]{1,0:T(8,128)(2,1)S(1)} %get-tuple-element.13), channel_id=1, source_target_pairs={{0,8},{8,0},{16,24},{24,16},{1,9},{9,1},{17,25},{25,17},{2,10},{10... | collective-permute-start | bytes 786440 | tf_op jit(solution)/shard_map/ppermute | solution.py:180
  49.1 4.0 %collective-permute-start.8 = (bf16[32,512]{1,0:T(8,128)(2,1)S(1)}, bf16[32,512]{1,0:T(8,128)(2,1)S(1)}, u32[]{:S(2)}, u32[]{:S(2)}) collective-permute-start(bf16[32,512]{1,0:T(8,128)(2,1)S(1)} %reduce_sum.12), channel_id=1, source_target_pairs={{0,16},{8,24},{16,0},{24,8},{1,17},{9,25},{17,1},{25,9},{2,18},{10... | collective-permute-start | bytes 98312 | tf_op jit(solution)/shard_map/ppermute | solution.py:180
  53.1 1.3 %collective-permute-start.9 = (bf16[32,512]{1,0:T(8,128)(2,1)S(1)}, bf16[32,512]{1,0:T(8,128)(2,1)S(1)}, u32[]{:S(2)}, u32[]{:S(2)}) collective-permute-start(bf16[32,512]{1,0:T(8,128)(2,1)S(1)} %fusion.mine_ref), channel_id=1, source_target_pairs={{0,8},{8,0},{16,24},{24,16},{1,9},{9,1},{17,25},{25,17},{2,10},{10... | collective-permute-start | bytes 98312 | tf_op jit(solution)/shard_map/ppermute | solution.py:180

commit v5 on v4

--- a/solution.py
+++ b/solution.py
@@ -182,7 +182,7 @@
 
 def gather_plan(size):
     far, mirror = size // 2, size - 2
-    wanted = [(mirror, 0), (1, 0), (2, 0), (far + 1, 1), (3, 2), (mirror + 1, mirror), (far, mirror)]
+    wanted = [(mirror, 0), (1, 0), (2, 0), (far + 1, 1), (far, mirror), (mirror + 1, mirror), (3, 2)]
     plan, held = [], {0}
     for mask, parent in wanted:
         if 0 < mask < size and mask not in held and parent in held:

time: 55.4 us -> 55.4 us (level)
  no operation moved by 1% of the time
where the time goes in v5:
time: 55.4 us; the launch traced here: 55.2 us
  starting transfers between devices  17.3 us (31%)
  waiting for transfers between devices  13.1 us (24%)
  blocking collectives  12.3 us (22%)
  Pallas kernels  10.4 us (19%)
  other arithmetic  0.81 us (1%)
  between operations  0.72 us (1%)
  local copies, waits for them, and re-layouts  0.67 us (1%)
    ppermute x10, starting transfers between devices, exchange(): return lax.ppermute(value, axis, [(i, i ^ mask) for i in range(size)])  17.3 us
    ppermute x10, waiting for transfers between devices, exchange(): return lax.ppermute(value, axis, [(i, i ^ mask) for i in range(size)])  13.1 us
    all_to_all x1, blocking collectives, per_device(): parts = lax.all_to_all(total, 'proc', 0, 0, tiled=True)  12.3 us
    pallas_call x1, Pallas kernels, grouped(): pl.pallas_call(functools.partial(group_kernel, ticks, anc_count), out_sha...  5.75 us
    pallas_call x1, Pallas kernels, solve(): pl.pallas_call(functools.partial(solve_kernel, ticks), out_shape=(jax.Sha...  2.31 us
    pallas_call x1, Pallas kernels, operators(): pl.pallas_call(operator_kernel, out_shape=jax.ShapeDtypeStruct((block + r...  1.4 us
  transfers between devices with their start and end apart: 10, of which 7 were waited for; matrix products, arithmetic and copies ran while one was open for 2% of the time, Pallas kernels for 10%

profile of v5, /device:TPU:0, one launch (start us, length us, event | category | flops | bytes accessed | tf_op | source)
XLA Modules:
  0.0 55.2 jit_solution(9276803455437300237)
XLA Ops:
  0.6 0.0 copy-start.1
  0.6 1.4 %operators.1.refs_0_ = bf16[512,256]{1,0:T(8,128)(2,1)S(1)} custom-call(bf16[256,256]{1,0:T(8,128)(2,1)} %diag_ref.1, bf16[256,256]{1,0:T(8,128)(2,1)} %chain_ref.1, bf16[256,256]{1,0:T(8,128)(2,1)} %rhs_ref.1), custom_call_target="tpu_custom_call" | custom-call | tf_op jit(solution)/shard_map/operators/pallas_call | solution.py:42
  2.0 0.0 copy-start.2
  2.1 3.0 %collective-permute-start = (bf16[512,256]{1,0:T(8,128)(2,1)S(1)}, bf16[512,256]{1,0:T(8,128)(2,1)S(1)}, u32[]{:S(2)}, u32[]{:S(2)}) collective-permute-start(bf16[512,256]{1,0:T(8,128)(2,1)S(1)} %operators.1.refs_0_), channel_id=1, source_target_pairs={{0,1},{1,0},{2,3},{3,2},{4,5},{5,4},{6,7},{7,6},{8,9},{9,8},{10,11... | collective-permute-start | bytes 786440 | tf_op jit(solution)/shard_map/ppermute | solution.py:180
  5.1 3.6 %collective-permute-start.3 = (bf16[512,256]{1,0:T(8,128)(2,1)S(1)}, bf16[512,256]{1,0:T(8,128)(2,1)S(1)}, u32[]{:S(2)}, u32[]{:S(2)}) collective-permute-start(bf16[512,256]{1,0:T(8,128)(2,1)S(1)} %operators.1.refs_0_), channel_id=1, source_target_pairs={{0,6},{1,7},{2,4},{3,5},{4,2},{5,3},{6,0},{7,1},{8,14},{9,15},{10,... | collective-permute-start | bytes 786440 | tf_op jit(solution)/shard_map/ppermute | solution.py:180
  8.7 0.0 collective-permute-start.1
  8.7 0.7 %add_bitcast_fusion.pair_ref = s32[80]{0:T(128)S(1)} fusion(s32[1,80]{1,0:T(1,128)} %param.14, s32[1,80]{1,0:T(1,128)} %param.15), kind=kLoop, calls=%fused_computation.4 | loop fusion | flops 160 | bytes 960 | tf_op jit(solution)/shard_map/add | solution.py:232
  9.4 0.0 copy-start
  9.4 5.8 %grouped.1.group_ref = bf16[1536,1024]{1,0:T(8,128)(2,1)S(1)} custom-call(s32[80]{0:T(128)S(1)} %add_bitcast_fusion.pair_ref, bf16[20480,256]{1,0:T(8,128)(2,1)} %factor_ref.1), custom_call_target="tpu_custom_call" | custom-call | flops 5242880 | bytes 10485760 | tf_op jit(solution)/shard_map/grouped/pallas_call | solution.py:83
  15.1 0.0 collective-permute-done.refs_1_
  15.1 0.8 %collective-permute-start.5 = (bf16[512,256]{1,0:T(8,128)(2,1)S(1)}, bf16[512,256]{1,0:T(8,128)(2,1)S(1)}, u32[]{:S(2)}, u32[]{:S(2)}) collective-permute-start(bf16[512,256]{1,0:T(8,128)(2,1)S(1)} %collective-permute-done.refs_1_), channel_id=1, source_target_pairs={{0,4},{1,5},{2,6},{3,7},{4,0},{5,1},{6,2},{7,3},{8,12},{9,13},{10,... | collective-permute-start | bytes 786440 | tf_op jit(solution)/shard_map/ppermute | solution.py:180
  16.0 0.2 collective-permute-done.3.refs_6_
  16.2 6.1 %collective-permute-start.4 = (bf16[512,256]{1,0:T(8,128)(2,1)S(1)}, bf16[512,256]{1,0:T(8,128)(2,1)S(1)}, u32[]{:S(2)}, u32[]{:S(2)}) collective-permute-start(bf16[512,256]{1,0:T(8,128)(2,1)S(1)} %collective-permute-done.3.refs_6_), channel_id=1, source_target_pairs={{0,2},{1,3},{2,0},{3,1},{4,6},{5,7},{6,4},{7,5},{8,10},{9,11},{10,... | collective-permute-start | bytes 786440 | tf_op jit(solution)/shard_map/ppermute | solution.py:180
  22.3 0.4 collective-permute-start.6
  22.7 0.0 collective-permute-done.1.refs_2_
  22.7 1.6 %collective-permute-start.2 = (bf16[512,256]{1,0:T(8,128)(2,1)S(1)}, bf16[512,256]{1,0:T(8,128)(2,1)S(1)}, u32[]{:S(2)}, u32[]{:S(2)}) collective-permute-start(bf16[512,256]{1,0:T(8,128)(2,1)S(1)} %collective-permute-done.1.refs_2_), channel_id=1, source_target_pairs={{0,1},{1,0},{2,3},{3,2},{4,5},{5,4},{6,7},{7,6},{8,9},{9,8},{10,11... | collective-permute-start | bytes 786440 | tf_op jit(solution)/shard_map/ppermute | solution.py:180
  24.3 6.5 %collective-permute-done.5.refs_5_ = bf16[512,256]{1,0:T(8,128)(2,1)S(1)} collective-permute-done((bf16[512,256]{1,0:T(8,128)(2,1)S(1)}, bf16[512,256]{1,0:T(8,128)(2,1)S(1)}, u32[]{:S(2)}, u32[]{:S(2)}) %collective-permute-start.5) | collective-permute-done | bytes 262176 | tf_op jit(solution)/shard_map/ppermute | solution.py:180
  30.8 0.8 %collective-permute-done.4.refs_4_ = bf16[512,256]{1,0:T(8,128)(2,1)S(1)} collective-permute-done((bf16[512,256]{1,0:T(8,128)(2,1)S(1)}, bf16[512,256]{1,0:T(8,128)(2,1)S(1)}, u32[]{:S(2)}, u32[]{:S(2)}) %collective-permute-start.4) | collective-permute-done | bytes 262176 | tf_op jit(solution)/shard_map/ppermute | solution.py:180
  31.7 0.0 collective-permute-done.6.refs_7_
  31.7 1.0 %collective-permute-done.2.refs_3_ = bf16[512,256]{1,0:T(8,128)(2,1)S(1)} collective-permute-done((bf16[512,256]{1,0:T(8,128)(2,1)S(1)}, bf16[512,256]{1,0:T(8,128)(2,1)S(1)}, u32[]{:S(2)}, u32[]{:S(2)}) %collective-permute-start.2) | collective-permute-done | bytes 262176 | tf_op jit(solution)/shard_map/ppermute | solution.py:180
  32.7 0.0 copy-done.1
  32.7 2.3 %solve.1 = (bf16[256,1536]{1,0:T(8,128)(2,1)S(1)}, bf16[256,512]{1,0:T(8,128)(2,1)S(1)}, f32[256,512]{1,0:T(8,128)S(1)}) custom-call(s32[1,6]{1,0:T(1,128)S(1)} %copy-done.1, bf16[1536,1024]{1,0:T(8,128)(2,1)S(1)} %grouped.1.group_ref, bf16[512,256]{1,0:T(8,128)(2,1)S(1)} %operators.1.refs_0_, bf16[512,256]{1,0:T(8,128)(2,1)S(1)} %collective-permute-done.refs_1_, ...), custom_call_target="tpu_custom_call" | custom-call | tf_op jit(solution)/shard_map/solve/pallas_call | solution.py:135
  35.0 0.1 collective-permute-start.7
  35.1 1.5 %collective-permute-done.7 = bf16[256,512]{1,0:T(8,128)(2,1)S(1)} collective-permute-done((bf16[256,512]{1,0:T(8,128)(2,1)S(1)}, bf16[256,512]{1,0:T(8,128)(2,1)S(1)}, u32[]{:S(2)}, u32[]{:S(2)}) %collective-permute-start.7) | collective-permute-done | bytes 262176 | tf_op jit(solution)/shard_map/ppermute | solution.py:180
  36.6 0.1 add_convert_fusion
  36.7 12.3 %all_to_all.12 = bf16[8,32,512]{2,1,0:T(8,128)(2,1)S(1)} all-to-all(bf16[8,32,512]{2,1,0:T(8,128)(2,1)S(1)} %bitcast.12), channel_id=1, replica_groups=mesh['layer'=4,'proc'=8] {'proc'}, dimensions={0} | all-to-all | bytes 524288 | tf_op jit(solution)/shard_map/all_to_all | solution.py:237
  49.1 1.6 %collective-permute-start.8 = (bf16[32,512]{1,0:T(8,128)(2,1)S(1)}, bf16[32,512]{1,0:T(8,128)(2,1)S(1)}, u32[]{:S(2)}, u32[]{:S(2)}) collective-permute-start(bf16[32,512]{1,0:T(8,128)(2,1)S(1)} %reduce_sum.12), channel_id=1, source_target_pairs={{0,16},{8,24},{16,0},{24,8},{1,17},{9,25},{17,1},{25,9},{2,18},{10... | collective-permute-start | bytes 98312 | tf_op jit(solution)/shard_map/ppermute | solution.py:180
  50.6 2.4 %collective-permute-done.8 = bf16[32,512]{1,0:T(8,128)(2,1)S(1)} collective-permute-done((bf16[32,512]{1,0:T(8,128)(2,1)S(1)}, bf16[32,512]{1,0:T(8,128)(2,1)S(1)}, u32[]{:S(2)}, u32[]{:S(2)}) %collective-permute-start.8) | collective-permute-done | bytes 32800 | tf_op jit(solution)/shard_map/ppermute | solution.py:180
  53.0 0.0 copy-done.2
  53.1 0.1 collective-permute-start.9
  53.1 0.7 %dynamic-slice_bitcast_fusion = bf16[1536,32]{0,1:T(8,128)(2,1)} fusion(bf16[256,1536]{1,0:T(8,128)(2,1)S(1)} %get-tuple-element.14, s32[]{:T(128)S(6)} %select_n.13), kind=kLoop, calls=%fused_computation.1 | loop fusion | bytes 196612 | tf_op jit(solution)/shard_map/transpose | solution.py:246
  53.8 0.5 collective-permute-done.9.other_ref
  54.3 0.0 copy-done
  54.3 0.9 %ancestor.1 = f32[32,1024]{1,0:T(8,128)} custom-call(bf16[32,512]{1,0:T(8,128)(2,1)S(1)} %fusion.mine_ref, bf16[32,512]{1,0:T(8,128)(2,1)S(1)} %collective-permute-done.9.other_ref, bf16[1024,256]{1,0:T(8,128)(2,1)S(1)} %copy-done), custom_call_target="tpu_custom_call" | custom-call | tf_op jit(solution)/shard_map/ancestor/pallas_call | solution.py:169
  (2 shorter events, 0.1 us)
Async XLA Ops:
  0.6 32.1 %copy-start.1 = (s32[1,6]{1,0:T(1,128)S(1)}, s32[1,6]{1,0:T(1,128)}, u32[]{:S(2)}) copy-start(s32[1,6]{1,0:T(1,128)} %owner_ref.1) | copy-start | bytes 76
  2.0 51.0 %copy-start.2 = (f32[1024,32]{0,1:T(8,128)S(1)}, f32[1024,32]{0,1:T(8,128)}, u32[]{:S(2)}) copy-start(f32[1024,32]{0,1:T(8,128)} %param.16) | copy-start | bytes 393220
  2.1 13.1 %collective-permute-start = (bf16[512,256]{1,0:T(8,128)(2,1)S(1)}, bf16[512,256]{1,0:T(8,128)(2,1)S(1)}, u32[]{:S(2)}, u32[]{:S(2)}) collective-permute-start(bf16[512,256]{1,0:T(8,128)(2,1)S(1)} %operators.1.refs_0_), channel_id=1, source_target_pairs={{0,1},{1,0},{2,3},{3,2},{4,5},{5,4},{6,7},{7,6},{8,9},{9,8},{10,11... | collective-permute-start | bytes 786440 | tf_op jit(solution)/shard_map/ppermute | solution.py:180
  5.1 11.1 %collective-permute-start.3 = (bf16[512,256]{1,0:T(8,128)(2,1)S(1)}, bf16[512,256]{1,0:T(8,128)(2,1)S(1)}, u32[]{:S(2)}, u32[]{:S(2)}) collective-permute-start(bf16[512,256]{1,0:T(8,128)(2,1)S(1)} %operators.1.refs_0_), channel_id=1, source_target_pairs={{0,6},{1,7},{2,4},{3,5},{4,2},{5,3},{6,0},{7,1},{8,14},{9,15},{10,... | collective-permute-start | bytes 786440 | tf_op jit(solution)/shard_map/ppermute | solution.py:180
  8.7 14.0 %collective-permute-start.1 = (bf16[512,256]{1,0:T(8,128)(2,1)S(1)}, bf16[512,256]{1,0:T(8,128)(2,1)S(1)}, u32[]{:S(2)}, u32[]{:S(2)}) collective-permute-start(bf16[512,256]{1,0:T(8,128)(2,1)S(1)} %operators.1.refs_0_), channel_id=1, source_target_pairs={{0,2},{1,3},{2,0},{3,1},{4,6},{5,7},{6,4},{7,5},{8,10},{9,11},{10,... | collective-permute-start | bytes 786440 | tf_op jit(solution)/shard_map/ppermute | solution.py:180
  9.4 45.0 %copy-start = (bf16[1024,256]{1,0:T(8,128)(2,1)S(1)}, bf16[1024,256]{1,0:T(8,128)(2,1)}, u32[]{:S(2)}) copy-start(bf16[1024,256]{1,0:T(8,128)(2,1)} %inverse_ref.1) | copy-start | bytes 1572868
  15.1 15.7 %collective-permute-start.5 = (bf16[512,256]{1,0:T(8,128)(2,1)S(1)}, bf16[512,256]{1,0:T(8,128)(2,1)S(1)}, u32[]{:S(2)}, u32[]{:S(2)}) collective-permute-start(bf16[512,256]{1,0:T(8,128)(2,1)S(1)} %collective-permute-done.refs_1_), channel_id=1, source_target_pairs={{0,4},{1,5},{2,6},{3,7},{4,0},{5,1},{6,2},{7,3},{8,12},{9,13},{10,... | collective-permute-start | bytes 786440 | tf_op jit(solution)/shard_map/ppermute | solution.py:180
  16.2 15.5 %collective-permute-start.4 = (bf16[512,256]{1,0:T(8,128)(2,1)S(1)}, bf16[512,256]{1,0:T(8,128)(2,1)S(1)}, u32[]{:S(2)}, u32[]{:S(2)}) collective-permute-start(bf16[512,256]{1,0:T(8,128)(2,1)S(1)} %collective-permute-done.3.refs_6_), channel_id=1, source_target_pairs={{0,2},{1,3},{2,0},{3,1},{4,6},{5,7},{6,4},{7,5},{8,10},{9,11},{10,... | collective-permute-start | bytes 786440 | tf_op jit(solution)/shard_map/ppermute | solution.py:180
  22.3 9.4 %collective-permute-start.6 = (bf16[512,256]{1,0:T(8,128)(2,1)S(1)}, bf16[512,256]{1,0:T(8,128)(2,1)S(1)}, u32[]{:S(2)}, u32[]{:S(2)}) collective-permute-start(bf16[512,256]{1,0:T(8,128)(2,1)S(1)} %collective-permute-done.3.refs_6_), channel_id=1, source_target_pairs={{0,1},{1,0},{2,3},{3,2},{4,5},{5,4},{6,7},{7,6},{8,9},{9,8},{10,11... | collective-permute-start | bytes 786440 | tf_op jit(solution)/shard_map/ppermute | solution.py:180
  22.7 10.0 %collective-permute-start.2 = (bf16[512,256]{1,0:T(8,128)(2,1)S(1)}, bf16[512,256]{1,0:T(8,128)(2,1)S(1)}, u32[]{:S(2)}, u32[]{:S(2)}) collective-permute-start(bf16[512,256]{1,0:T(8,128)(2,1)S(1)} %collective-permute-done.1.refs_2_), channel_id=1, source_target_pairs={{0,1},{1,0},{2,3},{3,2},{4,5},{5,4},{6,7},{7,6},{8,9},{9,8},{10,11... | collective-permute-start | bytes 786440 | tf_op jit(solution)/shard_map/ppermute | solution.py:180
  35.0 1.6 %collective-permute-start.7 = (bf16[256,512]{1,0:T(8,128)(2,1)S(1)}, bf16[256,512]{1,0:T(8,128)(2,1)S(1)}, u32[]{:S(2)}, u32[]{:S(2)}) collective-permute-start(bf16[256,512]{1,0:T(8,128)(2,1)S(1)} %get-tuple-element.13), channel_id=1, source_target_pairs={{0,8},{8,0},{16,24},{24,16},{1,9},{9,1},{17,25},{25,17},{2,10},{10... | collective-permute-start | bytes 786440 | tf_op jit(solution)/shard_map/ppermute | solution.py:180
  49.1 4.0 %collective-permute-start.8 = (bf16[32,512]{1,0:T(8,128)(2,1)S(1)}, bf16[32,512]{1,0:T(8,128)(2,1)S(1)}, u32[]{:S(2)}, u32[]{:S(2)}) collective-permute-start(bf16[32,512]{1,0:T(8,128)(2,1)S(1)} %reduce_sum.12), channel_id=1, source_target_pairs={{0,16},{8,24},{16,0},{24,8},{1,17},{9,25},{17,1},{25,9},{2,18},{10... | collective-permute-start | bytes 98312 | tf_op jit(solution)/shard_map/ppermute | solution.py:180
  53.1 1.3 %collective-permute-start.9 = (bf16[32,512]{1,0:T(8,128)(2,1)S(1)}, bf16[32,512]{1,0:T(8,128)(2,1)S(1)}, u32[]{:S(2)}, u32[]{:S(2)}) collective-permute-start(bf16[32,512]{1,0:T(8,128)(2,1)S(1)} %fusion.mine_ref), channel_id=1, source_target_pairs={{0,8},{8,0},{16,24},{24,16},{1,9},{9,1},{17,25},{25,17},{2,10},{10... | collective-permute-start | bytes 98312 | tf_op jit(solution)/shard_map/ppermute | solution.py:180
